TPU v7x, 32 devices: a whole 2x2x4 slice. The times are simulated.
32 devices in a mesh: node: 4 (over y, core), zero: 8 (over z, x).
Axes of the slice: x: 2, y: 2, z: 4, core: 2. Of those that a mesh axis runs over, the one named last changes fastest.
Arguments:
- grid_in: bfloat16 [8, 16, 360, 261], P('zero', 'node'), may hold values from -6 to 6
- target: float32 [8, 16, 360, 83], P('zero', 'node'), may hold values from -6 to 6
- noise_level: int32 [8], P('zero'), may hold values from 0 to 15
- land_mask: int32 [16, 360], P('node'), may hold values 0 or 1
- neighbours: int32 [3072, 16], P('node'), may hold values from 0 to 959
- halo_send: int32 [384], P('node'), may hold values from 0 to 767
- g2m: int32 [3072, 4], P('node'), may hold values from 0 to 1439
- m2g: int32 [5760, 3], P('node'), may hold values from 0 to 767
- legendre: float32 [16, 181, 181], P('node'), may hold values from -0.078125 to 0.078125
- w_attn: float32 [2048, 512], P(('node', 'zero')), may hold values from -0.25 to 0.25
- w_mlp: float32 [4096, 512], P(('node', 'zero')), may hold values from -0.25 to 0.25
- w_small: float32 [512, 512], P(('node', 'zero')), may hold values from -0.74278135 to 0.74278135
- mom_attn: float32 [2048, 512], P(('node', 'zero')), may hold values from -0.0078125 to 0.0078125
- mom_mlp: float32 [4096, 512], P(('node', 'zero')), may hold values from -0.0078125 to 0.0078125
- m_small: float32 [512, 512], P(('node', 'zero')), may hold values from -0.0008544922 to 0.0008544922
- v_small: float32 [512, 512], P(('node', 'zero')), may hold values from 1.5434852e-08 to 6.162203e-08
- ema_attn: float32 [2048, 512], P(('node', 'zero')), may hold values from -0.25 to 0.25
- ema_mlp: float32 [4096, 512], P(('node', 'zero')), may hold values from -0.25 to 0.25
- ema_small: float32 [512, 512], P(('node', 'zero')), may hold values from -0.375 to 0.375
Outputs:
- loss: float32 [], replicated
- clip_norm: float32 [], replicated
- new_attn: float32 [2048, 512], P(('node', 'zero'))
- new_mlp: float32 [4096, 512], P(('node', 'zero'))
- new_small: float32 [512, 512], P(('node', 'zero'))
- new_mom_attn: float32 [2048, 512], P(('node', 'zero'))
- new_mom_mlp: float32 [4096, 512], P(('node', 'zero'))
- new_m_small: float32 [512, 512], P(('node', 'zero'))
- new_v_small: float32 [512, 512], P(('node', 'zero'))
- new_ema_attn: float32 [2048, 512], P(('node', 'zero'))
- new_ema_mlp: float32 [4096, 512], P(('node', 'zero'))
- new_ema_small: float32 [512, 512], P(('node', 'zero'))
Inputs may be any that keep to these rules, and one draw needn't show every extreme that they name: `neighbours`: in the neighbour lists of node block b, a value below 768 names a node of block b, 768 + i the i-th halo_send entry of block b-1, 864 + i that of block b+1 (cyclic); g2m names pixels of the same block, m2g nodes of the same block.
All inputs are finite; a program needn't handle non-finite values. No bound on the sum of `land_mask` on one device may be relied on, other than what follows from the above.
Results may differ from a plain program's by a relative error of at most 0.0068.
The roundings to bfloat16 on the way count: a program that leaves them out, or rounds other values in their place, can miss the bound.
Values may be sent and summed in bfloat16 or wider, within the bound.
A program may use at most 384 MiB of HBM per device.

v0:
```python
import math

import jax
import jax.numpy as jnp
from jax import lax
from jax.sharding import PartitionSpec as P

HEAD_COUNT = 4
NOISE_FEATS = 42
LEVELS = 16
NS_ITERS = 3
STEP = 10


top_precision = lax.Precision.HIGHEST
norm_epsilon = 1e-05
trace_epsilon = 1e-12
clip_limit = 1.0
moment_decay = 0.95
orthogonal_rate = 0.1
adam_first = 0.9
adam_second = 0.95
adam_rate = 0.02
adam_epsilon = 1e-08
average_decay = 0.9
newton_first = 3.4445
newton_second = -4.775
newton_third = 2.0315
sigma_lowest = 0.1
sigma_highest = 20.0


def padded(cells, sides, width):
    for axis, dim in sides:
        count = lax.axis_size(axis)
        head = lax.slice_in_dim(cells, 0, width, axis=dim)
        tail = lax.slice_in_dim(cells, cells.shape[dim] - width, cells.shape[dim], axis=dim)
        cells = jnp.concatenate(
            [
                lax.ppermute(tail, axis, [(i, (i + 1) % count) for i in range(count)]),
                cells,
                lax.ppermute(head, axis, [((i + 1) % count, i) for i in range(count)]),
            ],
            axis=dim,
        )
    return cells


def passed_along(value, axis, steps):
    count = lax.axis_size(axis)
    pairs = [(source, (source + steps) % count) for source in range(count)]
    return lax.ppermute(value, axis, pairs)


def noise_scalars(level):
    sigma = sigma_lowest * (sigma_highest / sigma_lowest) ** (
        level.astype(jnp.float32) / (LEVELS - 1)
    )
    total = sigma * sigma + 1.0
    return (sigma, lax.rsqrt(total), 1.0 / total, sigma * lax.rsqrt(total), total / (sigma * sigma))


def noise_features(sigma):
    half_count = NOISE_FEATS // 2
    frequency = jnp.exp(jnp.arange(half_count).astype(jnp.float32) * (3.0 / half_count))
    phases = 0.25 * jnp.log(sigma) * frequency
    return jnp.concatenate([jnp.sin(phases), jnp.cos(phases)])


def cond_norm(value_rows, gain_shift, bias_shift):
    centred = value_rows - jnp.mean(value_rows, axis=-1, keepdims=True)
    spread = jnp.mean(centred * centred, axis=-1, keepdims=True)
    return centred * lax.rsqrt(spread + norm_epsilon) * (1.0 + gain_shift) + bias_shift


def ns_basis(gram_matrix):
    score_scale = lax.rsqrt(jnp.trace(gram_matrix) + trace_epsilon)
    current = gram_matrix * (score_scale * score_scale)
    identity = jnp.eye(gram_matrix.shape[0], dtype=jnp.float32)
    basis = identity
    for iteration in range(NS_ITERS):
        squared = jnp.dot(current, current, precision=top_precision)
        polynomial = newton_first * identity + newton_second * current + newton_third * squared
        basis = jnp.dot(basis, polynomial, precision=top_precision)
        if iteration + 1 < NS_ITERS:
            current = jnp.dot(
                polynomial,
                jnp.dot(current, polynomial, precision=top_precision),
                precision=top_precision,
            )
    return (basis, score_scale)


def dot_left(left, right):
    return lax.dot_general(
        left, right, (((0,), (0,)), ((), ())), preferred_element_type=jnp.float32
    )


def dot_right(left, right):
    return lax.dot_general(
        left, right, (((1,), (1,)), ((), ())), preferred_element_type=jnp.float32
    )


def scatter_mean(value_rows, index, count):
    spread = jnp.broadcast_to(
        value_rows[:, None, :] / index.shape[1], index.shape + (value_rows.shape[1],)
    )
    return jnp.zeros((count, value_rows.shape[1]), jnp.float32).at[index].add(spread)


def split_weights(gathered, cin, channels):
    attn_full, mlp_full, small_full = gathered
    width = attn_full.shape[1]
    half = mlp_full.shape[0] // 2
    return (
        attn_full[: 3 * width],
        attn_full[3 * width :],
        mlp_full[:half],
        mlp_full[half:],
        small_full[:cin],
        small_full[cin : cin + channels],
        small_full[cin + channels :].reshape(4, -1, width),
    )


def forward(weights, grid_in, noise_level, neighbours, halo_send, g2m, m2g):
    w_query, w_output, w_upper, w_down, w_enc, w_dec, w_cond = weights
    width = w_output.shape[1]
    rows, fanout = neighbours.shape
    halo_rows = halo_send.shape[0]
    cin = grid_in.shape[-1]
    channels = w_dec.shape[0]
    sigma, c_input, c_skip, c_output, loss_weight = noise_scalars(noise_level[0])
    scale_input = jnp.where(jnp.arange(cin) < channels, c_input, 1.0)
    inputs = (grid_in[0].reshape(-1, cin).astype(jnp.float32) * scale_input).astype(jnp.bfloat16)
    embedded = jnp.dot(inputs, w_enc, preferred_element_type=jnp.float32)
    stream_in = jnp.mean(embedded[g2m], axis=1)
    features = noise_features(sigma).astype(jnp.bfloat16)
    modulation = jnp.einsum("f,jfd->jd", features, w_cond, preferred_element_type=jnp.float32)
    first = cond_norm(stream_in, modulation[0], modulation[1]).astype(jnp.bfloat16)
    packed = dot_right(first, w_query).astype(jnp.bfloat16)
    query_rows = packed[:, :width].reshape(rows, HEAD_COUNT, -1)
    pairs = packed[:, width:]
    borrowed = padded(pairs[halo_send], (("node", 0),), halo_rows)
    extended = jnp.concatenate([pairs, borrowed[:halo_rows], borrowed[2 * halo_rows :]], axis=0)
    picked = extended[neighbours]
    key_rows = picked[:, :, :width].reshape(rows, fanout, HEAD_COUNT, -1)
    value_rows = picked[:, :, width:].reshape(rows, fanout, HEAD_COUNT, -1)
    score_scale = query_rows.shape[-1] ** (-0.5)
    attention_logits = (
        jnp.einsum("out,ovut->ouv", query_rows, key_rows, preferred_element_type=jnp.float32)
        * score_scale
    )
    attention_probabilities = jax.nn.softmax(attention_logits, axis=-1)
    probabilities_reduced = attention_probabilities.astype(jnp.bfloat16)
    blended_values = jnp.einsum(
        "iqa,iaqz->iqz", probabilities_reduced, value_rows, preferred_element_type=jnp.float32
    )
    blended_values = blended_values.reshape(rows, width).astype(jnp.bfloat16)
    stream_mid = stream_in + dot_right(blended_values, w_output)
    second = cond_norm(stream_mid, modulation[2], modulation[3]).astype(jnp.bfloat16)
    upper = dot_right(second, w_upper)
    activ = jax.nn.gelu(upper).astype(jnp.bfloat16)
    stream_out = stream_mid + jnp.dot(activ, w_down, preferred_element_type=jnp.float32)
    latent = jnp.mean(stream_out[m2g], axis=1).astype(jnp.bfloat16)
    network = dot_right(latent, w_dec)
    saved_cache = {
        "inputs": inputs,
        "stream_in": stream_in,
        "features": features,
        "modulation": modulation,
        "first": first,
        "queries": query_rows,
        "keys": key_rows,
        "values": value_rows,
        "probs": attention_probabilities,
        "probs_low": probabilities_reduced,
        "mixed": blended_values,
        "stream_mid": stream_mid,
        "second": second,
        "upper": upper,
        "activ": activ,
        "latent": latent,
    }
    return (network, saved_cache)


def spectral(network, grid_in, target, keep_mask, legendre, noise_level):
    sigma, c_input, c_skip, c_output, loss_weight = noise_scalars(noise_level[0])
    lat_rows, lon_count, channels = target.shape[1:]
    modes, degrees = legendre.shape[1:]
    node_count = lax.axis_size("node")
    predicted = c_skip * grid_in[0, :, :, :channels].astype(
        jnp.float32
    ) + c_output * network.reshape(lat_rows, lon_count, channels)
    error = (predicted - target[0]) * keep_mask
    turns = jnp.arange(lon_count)[:, None] * jnp.arange(modes)[None, :] % lon_count
    phases = turns.astype(jnp.float32) * (2.0 * math.pi / lon_count)
    cosine = jnp.cos(phases)
    sine = jnp.sin(phases)
    parts = jnp.stack(
        [
            jnp.einsum("tnc,nm->tmc", error, cosine, precision=top_precision),
            -jnp.einsum("tnc,nm->tmc", error, sine, precision=top_precision),
        ]
    )
    weight = loss_weight / (2 * modes * degrees * channels)
    padded_degrees = -(-degrees // node_count) * node_count
    partial_coeffs = jnp.einsum("tml,rtmc->rmlc", legendre, parts, precision=top_precision)
    partial_coeffs = jnp.pad(
        partial_coeffs, ((0, 0), (0, 0), (0, padded_degrees - degrees), (0, 0))
    )
    share = lax.psum_scatter(
        partial_coeffs.astype(jnp.bfloat16), "node", scatter_dimension=2, tiled=True
    ).astype(jnp.float32)
    loss_here = weight * jnp.sum(share * share)
    coeffs_grad = lax.all_gather(
        (2.0 * weight * share).astype(jnp.bfloat16), "node", axis=2, tiled=True
    ).astype(jnp.float32)[:, :, :degrees]
    grad_parts = jnp.einsum("tml,rmlc->rtmc", legendre, coeffs_grad, precision=top_precision)
    grad_error = jnp.einsum(
        "tmc,nm->tnc", grad_parts[0], cosine, precision=top_precision
    ) - jnp.einsum("tmc,nm->tnc", grad_parts[1], sine, precision=top_precision)
    grad_network = (grad_error * keep_mask * c_output).reshape(lat_rows * lon_count, channels)
    return (loss_here, grad_network.astype(jnp.bfloat16))


def backward(weights, saved_cache, grad_network, neighbours, halo_send, g2m, m2g):
    w_query, w_output, w_upper, w_down, w_enc, w_dec, w_cond = weights
    width = w_output.shape[1]
    rows, fanout = neighbours.shape
    halo_rows = halo_send.shape[0]
    pixel_rows = m2g.shape[0]
    g_dec = dot_left(grad_network, saved_cache["latent"])
    grad_latent = jnp.dot(grad_network, w_dec, preferred_element_type=jnp.float32)
    grad_out = scatter_mean(grad_latent, m2g, rows)
    grad_branch = grad_out.astype(jnp.bfloat16)
    g_down = dot_left(saved_cache["activ"], grad_branch)
    grad_activ = dot_right(grad_branch, w_down)
    gelu_value, gelu_back = jax.vjp(jax.nn.gelu, saved_cache["upper"])
    grad_upper = gelu_back(grad_activ)[0].astype(jnp.bfloat16)
    g_upper = dot_left(grad_upper, saved_cache["second"])
    grad_second = jnp.dot(grad_upper, w_upper, preferred_element_type=jnp.float32)
    modulation = saved_cache["modulation"]
    norm_value, norm_back = jax.vjp(
        cond_norm, saved_cache["stream_mid"], modulation[2], modulation[3]
    )
    grad_mid_norm, grad_gain_two, grad_bias_two = norm_back(grad_second)
    grad_mid = grad_out + grad_mid_norm
    grad_attn = grad_mid.astype(jnp.bfloat16)
    g_output = dot_left(grad_attn, saved_cache["mixed"])
    gradient_blended = jnp.dot(grad_attn, w_output, preferred_element_type=jnp.float32)
    gradient_blended = gradient_blended.astype(jnp.bfloat16).reshape(rows, HEAD_COUNT, -1)
    attention_probabilities = saved_cache["probs"]
    score_scale = saved_cache["queries"].shape[-1] ** (-0.5)
    grad_probs = jnp.einsum(
        "out,ovut->ouv", gradient_blended, saved_cache["values"], preferred_element_type=jnp.float32
    )
    gradient_logits = attention_probabilities * (
        grad_probs - jnp.sum(attention_probabilities * grad_probs, axis=-1, keepdims=True)
    )
    gradient_logits = gradient_logits.astype(jnp.bfloat16)
    grad_queries = (
        jnp.einsum(
            "iqa,iaqz->iqz",
            gradient_logits,
            saved_cache["keys"],
            preferred_element_type=jnp.float32,
        )
        * score_scale
    )
    grad_keys = (
        jnp.einsum(
            "zuf,zua->zfua",
            gradient_logits,
            saved_cache["queries"],
            preferred_element_type=jnp.float32,
        )
        * score_scale
    )
    grad_values = jnp.einsum(
        "zuf,zua->zfua",
        saved_cache["probs_low"],
        gradient_blended,
        preferred_element_type=jnp.float32,
    )
    grad_picked = jnp.concatenate(
        [grad_keys.reshape(rows, fanout, width), grad_values.reshape(rows, fanout, width)], axis=-1
    )
    grad_extended = (
        jnp.zeros((rows + 2 * halo_rows, 2 * width), jnp.float32).at[neighbours].add(grad_picked)
    )
    from_upper = passed_along(
        grad_extended[rows : rows + halo_rows].astype(jnp.bfloat16), "node", -1
    ).astype(jnp.float32)
    from_lower = passed_along(
        grad_extended[rows + halo_rows :].astype(jnp.bfloat16), "node", 1
    ).astype(jnp.float32)
    grad_pairs = grad_extended[:rows].at[halo_send].add(from_upper + from_lower)
    grad_packed = jnp.concatenate([grad_queries.reshape(rows, width), grad_pairs], axis=-1).astype(
        jnp.bfloat16
    )
    g_query = dot_left(grad_packed, saved_cache["first"])
    grad_first = jnp.dot(grad_packed, w_query, preferred_element_type=jnp.float32)
    norm_value, norm_back = jax.vjp(
        cond_norm, saved_cache["stream_in"], modulation[0], modulation[1]
    )
    grad_in_norm, grad_gain_one, grad_bias_one = norm_back(grad_first)
    grad_in = grad_mid + grad_in_norm
    grad_modulation = jnp.stack([grad_gain_one, grad_bias_one, grad_gain_two, grad_bias_two])
    g_cond = jnp.einsum(
        "f,jd->jfd", saved_cache["features"].astype(jnp.float32), grad_modulation
    ).reshape(-1, width)
    grad_embedded = scatter_mean(grad_in, g2m, pixel_rows).astype(jnp.bfloat16)
    g_enc = dot_left(saved_cache["inputs"], grad_embedded)
    return (
        jnp.concatenate([g_query, g_output], axis=0),
        jnp.concatenate([g_upper, g_down], axis=0),
        jnp.concatenate([g_enc, g_dec, g_cond], axis=0),
    )


def gram_of(left, right):
    return jnp.dot(left.T, right, precision=top_precision)


def slotted(attn_piece, mlp_piece, attn_upper, mlp_upper):
    return jnp.stack(
        [
            attn_piece * (1.0 - attn_upper),
            attn_piece * attn_upper,
            mlp_piece * (1.0 - mlp_upper),
            mlp_piece * mlp_upper,
        ]
    )


def on_device(
    grid_in,
    target,
    noise_level,
    land_mask,
    neighbours,
    halo_send,
    g2m,
    m2g,
    legendre,
    w_attn,
    w_mlp,
    w_small,
    mom_attn,
    mom_mlp,
    m_small,
    v_small,
    ema_attn,
    ema_mlp,
    ema_small,
):
    cin = grid_in.shape[-1]
    channels = target.shape[-1]
    lowered = (
        w_attn.astype(jnp.bfloat16),
        w_mlp.astype(jnp.bfloat16),
        w_small.astype(jnp.bfloat16),
    )
    weights = split_weights(
        (
            lax.all_gather(lowered[0], ("node", "zero"), axis=0, tiled=True),
            lax.all_gather(lowered[1], ("node", "zero"), axis=0, tiled=True),
            lax.all_gather(lowered[2], ("node", "zero"), axis=0, tiled=True),
        ),
        cin,
        channels,
    )
    network, saved_cache = forward(weights, grid_in, noise_level, neighbours, halo_send, g2m, m2g)
    keep_mask = 1.0 - land_mask.astype(jnp.float32)[:, :, None] * (
        jnp.arange(channels) == channels - 1
    ).astype(jnp.float32)
    loss_here, grad_network = spectral(network, grid_in, target, keep_mask, legendre, noise_level)
    regathered = split_weights(
        (
            lax.all_gather(lowered[0], ("node", "zero"), axis=0, tiled=True),
            lax.all_gather(lowered[1], ("node", "zero"), axis=0, tiled=True),
            lax.all_gather(lowered[2], ("node", "zero"), axis=0, tiled=True),
        ),
        cin,
        channels,
    )
    network_again, cache_again = forward(
        regathered, grid_in, noise_level, neighbours, halo_send, g2m, m2g
    )
    local_grads = backward(regathered, cache_again, grad_network, neighbours, halo_send, g2m, m2g)
    g_attn, g_mlp, g_small = (
        lax.psum_scatter(local_grads[0], ("node", "zero"), scatter_dimension=0, tiled=True),
        lax.psum_scatter(local_grads[1], ("node", "zero"), scatter_dimension=0, tiled=True),
        lax.psum_scatter(local_grads[2], ("node", "zero"), scatter_dimension=0, tiled=True),
    )
    squares = jnp.sum(g_attn * g_attn) + jnp.sum(g_mlp * g_mlp) + jnp.sum(g_small * g_small)
    attn_rows, width = w_attn.shape
    mlp_rows = w_mlp.shape[0]
    mlp_half = mlp_rows * lax.axis_size(("node", "zero")) // 2
    flat_index = lax.axis_index(("node", "zero"))
    attn_upper = (flat_index * attn_rows >= 3 * width).astype(jnp.float32)
    mlp_upper = (flat_index * mlp_rows >= mlp_half).astype(jnp.float32)
    total_sq, loss = lax.psum((squares, loss_here), ("node", "zero"))
    clip_norm = jnp.sqrt(total_sq)
    factor = jnp.minimum(1.0, clip_limit / clip_norm)
    moment_attn = moment_decay * mom_attn + factor * g_attn
    moment_mlp = moment_decay * mom_mlp + factor * g_mlp
    grams = lax.psum(
        slotted(
            gram_of(moment_attn, moment_attn),
            gram_of(moment_mlp, moment_mlp),
            attn_upper,
            mlp_upper,
        ),
        ("node", "zero"),
    )
    attn_basis, attn_scale = ns_basis(jnp.where(attn_upper > 0.5, grams[1], grams[0]))
    mlp_basis, mlp_scale = ns_basis(jnp.where(mlp_upper > 0.5, grams[3], grams[2]))
    attn_factor = jnp.where(attn_upper > 0.5, 0.2 * math.sqrt(width), 0.2 * math.sqrt(3 * width))
    mlp_factor = 0.2 * math.sqrt(max(mlp_half, width))
    new_attn = w_attn - orthogonal_rate * attn_factor * jnp.dot(
        moment_attn * attn_scale, attn_basis, precision=top_precision
    )
    new_mlp = w_mlp - orthogonal_rate * mlp_factor * jnp.dot(
        moment_mlp * mlp_scale, mlp_basis, precision=top_precision
    )
    clipped = factor * g_small
    first_small = adam_first * m_small + (1.0 - adam_first) * clipped
    second_small = adam_second * v_small + (1.0 - adam_second) * clipped * clipped
    new_small = w_small - adam_rate * (first_small / (1.0 - adam_first**STEP)) / (
        jnp.sqrt(second_small / (1.0 - adam_second**STEP)) + adam_epsilon
    )
    return (
        loss,
        clip_norm,
        new_attn,
        new_mlp,
        new_small,
        moment_attn,
        moment_mlp,
        first_small,
        second_small,
        average_decay * ema_attn + (1.0 - average_decay) * new_attn,
        average_decay * ema_mlp + (1.0 - average_decay) * new_mlp,
        average_decay * ema_small + (1.0 - average_decay) * new_small,
    )


def solution(mesh):
    return jax.shard_map(
        on_device,
        mesh=mesh,
        in_specs=(
            P("zero", "node", None, None),
            P("zero", "node", None, None),
            P("zero"),
            P("node", None),
            P("node", None),
            P("node"),
            P("node", None),
            P("node", None),
            P("node", None, None),
            P(("node", "zero"), None),
            P(("node", "zero"), None),
            P(("node", "zero"), None),
            P(("node", "zero"), None),
            P(("node", "zero"), None),
            P(("node", "zero"), None),
            P(("node", "zero"), None),
            P(("node", "zero"), None),
            P(("node", "zero"), None),
            P(("node", "zero"), None),
        ),
        out_specs=(
            P(),
            P(),
            P(("node", "zero"), None),
            P(("node", "zero"), None),
            P(("node", "zero"), None),
            P(("node", "zero"), None),
            P(("node", "zero"), None),
            P(("node", "zero"), None),
            P(("node", "zero"), None),
            P(("node", "zero"), None),
            P(("node", "zero"), None),
            P(("node", "zero"), None),
        ),
        check_vma=False,
    )
```

profile of v0, /device:TPU:0, one launch (start us, length us, event | category | flops | bytes accessed | tf_op | source)
XLA Modules:
  0.0 1985.8 jit_solution(8019367942205110965)
XLA Ops:
  13.1 73.3 %all_gather.15 = bf16[512,512]{1,0:T(8,128)(2,1)S(1)} all-gather(bf16[16,512]{1,0:T(8,128)(2,1)S(1)} %convert_element_type.144), channel_id=1, replica_groups=mesh['node'=4,'zero'=8] {'node','zero'}, dimensions={0}, use_global_device_ids=true | all-gather | bytes 540672 | tf_op jit(solution)/shard_map/all_gather | solution.py:372
  95.2 15.6 gather_fusion
  110.8 7.5 reshape.192
  118.4 7.7 reduce_sum.196
  145.4 52.7 %gather_fusion.2 = bf16[12288,1024]{1,0:T(8,128)(2,1)} fusion(bf16[960,1024]{1,0:T(8,128)(2,1)S(1)} %pad_maximum_fusion.5, s32[12288]{0:T(1024)S(1)} %broadcast_clamp_fusion), kind=kCustom, calls=%fused_computation.2 | custom fusion | bytes 50380800 | tf_op jit(solution)/shard_map/gather | solution.py:148
  198.1 19.6 fusion.169
  217.7 4.5 copy-done.17
  222.2 7.6 fusion.8
  234.4 7.3 fusion.3
  258.3 12.6 gather_fusion.3
  270.9 13.9 reshape.216
  284.7 12.1 reduce_sum.205
  304.2 28.6 %convert_bitcast_fusion = bf16[2,181,181,83]{2,3,0,1:T(8,128)(2,1)} fusion(f32[2,4,181,83]{3,1,0,2:T(4,128)S(1)} %copy.102, f32[4,181,181]{2,0,1:T(4,128)S(1)} %copy-done), kind=kOutput, calls=%fused_computation.15 | convolution fusion | flops 266477984 | bytes 11881564 | tf_op jit(solution)/shard_map/tml,rtmc->rmlc/dot_general | solution.py:211
  332.7 41.8 %copy.137 = bf16[2,181,181,83]{1,0,3,2:T(2,128)(2,1)} copy(bf16[2,181,181,83]{2,3,0,1:T(8,128)(2,1)} %convert_bitcast_fusion) | data formatting | bytes 21753304
  374.6 18.5 pad.5.clone
  394.9 266.0 %all-reduce.8.cloned.1.call-done = bf16[2,181,184,83]{1,0,3,2:T(2,128)(2,1)} async-done(((bf16[2,181,184,83]{1,0,3,2:T(2,128)(2,1)}), bf16[2,181,184,83]{1,0,3,2:T(2,128)(2,1)}) %all-reduce.8.cloned.1.call-update) | async-done | bytes 11056944
  660.9 12.5 fusion.13
  676.3 19.0 reshape.174
  695.3 4.8 copy.112
  700.1 73.1 %all-gather.8.cloned.1.call-done = bf16[2,181,184,83]{1,0,3,2:T(2,128)(2,1)} async-done(((bf16[2,181,46,83]{1,0,3,2:T(2,128)(2,1)}), bf16[2,181,184,83]{1,0,3,2:T(2,128)(2,1)}) %all-gather.8.cloned.1.call-update) | async-done | bytes 11056944 | tf_op jit(solution)/shard_map/all_gather | solution.py:219
  773.3 13.6 slice.146
  786.9 41.9 %copy.135 = bf16[2,181,181,83]{2,3,0,1:T(8,128)(2,1)} copy(bf16[2,181,181,83]{1,0,3,2:T(2,128)(2,1)} %slice.146) | data formatting | bytes 21753304
  828.8 18.6 convolution_bitcast_fusion
  853.4 5.5 broadcast_in_dim.47
  858.9 14.3 reshape.223
  873.2 28.6 %scatter_custom_fusion = f32[768,512]{1,0:T(8,128)S(1)} fusion(s32[4320]{0:T(1024)} %copy-done.52, f32[4320,512]{1,0:T(8,128)} %reshape.223, f32[]{:T(128)} %constant.62.clone.1), kind=kCustom, calls=%fused_computation.148 | custom fusion | flops 2211840 | bytes 1573376 | tf_op jit(solution)/shard_map/scatter-add | solution.py:110
  903.5 7.8 fusion.20
  923.8 34.0 %multiply_reduce_fusion = (f32[768,4,16]{1,2,0:T(8,128)}, f32[768,16,4,128]{3,2,1,0:T(4,128)}) fusion(f32[768,4,128]{2,1,0:T(4,128)S(1)} %copy.136, bf16[768,16,4,128]{3,2,1,0:T(4,128)(2,1)} %reshape.174, f32[768,4,16]{1,2,0:T(8,128)} %copy.112), kind=kLoop, calls=%fused_computation.12 | loop fusion | flops 25116672 | bytes 39714816
  957.9 5.2 copy.131
  963.1 4.4 copy.110
  967.5 17.1 multiply_bitcast_fusion.1
  984.7 29.5 %reshape.177 = f32[768,16,512]{2,1,0:T(8,128)} reshape(f32[768,16,4,128]{3,2,1,0:T(4,128)} %multiply_bitcast_fusion.1) | data formatting | bytes 50331648 | tf_op jit(solution)/shard_map/reshape | solution.py:290
  1014.2 29.6 %reshape.178 = f32[768,16,512]{2,1,0:T(8,128)} reshape(f32[768,16,4,128]{3,2,1,0:T(4,128)} %get-tuple-element.38) | data formatting | bytes 50331648 | tf_op jit(solution)/shard_map/reshape | solution.py:290
  1043.8 34.1 %pad_maximum_fusion = f32[768,16,1024]{2,1,0:T(8,128)} fusion(f32[768,16,512]{2,1,0:T(8,128)} %reshape.178, f32[768,16,512]{2,1,0:T(8,128)} %reshape.177), kind=kLoop, calls=%fused_computation.11 | loop fusion | flops 12582912 | bytes 100663296 | tf_op jit(solution)/shard_map/concatenate | solution.py:289
  1077.8 108.2 %scatter_custom_fusion.1 = f32[960,1024]{1,0:T(8,128)} fusion(s32[12288]{0:T(1024)} %copy-done.44, f32[12288,1024]{1,0:T(8,128)} %bitcast.206, f32[]{:T(128)} %constant.62.clone.1), kind=kCustom, calls=%fused_computation.57 | custom fusion | flops 12582912 | bytes 3932672 | tf_op jit(solution)/shard_map/scatter-add | solution.py:293
  1194.2 9.7 fusion.6
  1213.2 5.2 scatter_custom_fusion.2
  1235.5 5.1 broadcast_in_dim.54
  1240.6 7.7 reshape.247
  1248.3 20.9 %scatter_custom_fusion.3 = f32[1440,512]{1,0:T(8,128)} fusion(s32[3072]{0:T(1024)} %copy-done.55, f32[3072,512]{1,0:T(8,128)} %reshape.247, f32[]{:T(128)} %constant.62.clone.1), kind=kCustom, calls=%fused_computation.83 | custom fusion | flops 1572864 | bytes 2949632 | tf_op jit(solution)/shard_map/scatter-add | solution.py:110
  1286.2 4.7 fusion.92
  1290.9 4.3 pad_maximum_fusion.1
  1296.0 113.0 %reduce-scatter.8.cloned.1.call-done = f32[16,512]{1,0:T(8,128)} async-done(((f32[512,512]{1,0:T(8,128)}), f32[16,512]{1,0:T(8,128)}) %reduce-scatter.8.cloned.1.call-update) | async-done | bytes 32784 | tf_op jit(solution)/shard_map/reduce_scatter | solution.py:398
  1410.4 140.8 %reduce-scatter.4.cloned.1.call-done = f32[64,512]{1,0:T(8,128)} async-done(((f32[2048,512]{1,0:T(8,128)}), f32[64,512]{1,0:T(8,128)}) %reduce-scatter.4.cloned.1.call-update) | async-done | bytes 131088 | tf_op jit(solution)/shard_map/reduce_scatter | solution.py:396
  1552.7 183.4 %reduce-scatter.6.cloned.1.call-done = f32[128,512]{1,0:T(8,128)} async-done(((f32[4096,512]{1,0:T(8,128)}), f32[128,512]{1,0:T(8,128)}) %reduce-scatter.6.cloned.1.call-update) | async-done | bytes 262160 | tf_op jit(solution)/shard_map/reduce_scatter | solution.py:397
  1739.7 40.3 %all-reduce.2 = (f32[]{:T(128)}, f32[]{:T(128)}) all-reduce(f32[]{:T(128)S(6)} %mul.650, f32[]{:T(128)S(6)} %add.259), channel_id=1, replica_groups=mesh['node'=4,'zero'=8] {'node','zero'}, use_global_device_ids=true, to_apply=%region_10.11 | all-reduce | flops 2 | bytes 16 | tf_op jit(solution)/shard_map/psum | solution.py:407
  1787.9 139.7 %all-reduce.6.cloned.1.call-done = f32[4,512,512]{2,1,0:T(8,128)} async-done(((f32[4,512,512]{2,1,0:T(8,128)}), f32[4,512,512]{2,1,0:T(8,128)}) %all-reduce.6.cloned.1.call-update) | async-done | bytes 4194320 | tf_op jit(solution)/shard_map/psum | solution.py:412
  1927.6 4.3 fusion.61
  (350 shorter events, 191.8 us)
Async XLA Ops:
  7.2 297.0 %copy-start = (f32[4,181,181]{2,0,1:T(4,128)S(1)}, f32[4,181,181]{2,0,1:T(4,128)}, u32[]{:S(2)}) copy-start(f32[4,181,181]{2,0,1:T(4,128)} %param.27) | copy-start | bytes 1572532
  7.2 80.3 %copy-start.74 = (s32[768,4]{0,1:T(4,128)S(1)}, s32[768,4]{0,1:T(4,128)}, u32[]{:S(2)}) copy-start(s32[768,4]{0,1:T(4,128)} %param.25) | copy-start | bytes 36868
  7.2 80.4 %copy-start.34 = (bf16[1,4,360,261]{2,1,3,0:T(4,128)(2,1)S(1)}, bf16[1,4,360,261]{2,1,3,0:T(4,128)(2,1)}, u32[]{:S(2)}) copy-start(bf16[1,4,360,261]{2,1,3,0:T(4,128)(2,1)} %param.19) | copy-start | bytes 2255044
  7.2 121.7 %all-gather.4.cloned.1.call-start = ((), (), s32[]{:S(2)}) async-start(), calls=%async_computation.3 | async-start | bytes 2162688 | tf_op jit(solution)/shard_map/all_gather | solution.py:370
  8.9 236.8 %all-gather.6.cloned.1.call-start = ((), (), s32[]{:S(2)}) async-start(), calls=%async_computation.4 | async-start | bytes 4325376 | tf_op jit(solution)/shard_map/all_gather | solution.py:371
  10.6 78.7 %copy-start.75 = (s32[4,360]{1,0:T(4,128)S(1)}, s32[4,360]{1,0:T(4,128)}, u32[]{:S(2)}) copy-start(s32[4,360]{1,0:T(4,128)} %param.22) | copy-start | bytes 17284
  10.6 650.3 %all-reduce.8.cloned.1.call-start = ((), (), s32[]{:S(2)}) async-start(), calls=%async_computation.10 | async-start | bytes 31277056
  11.5 75.8 %copy-start.81 = (bf16[21]{0:T(256)(128)(2,1)}, bf16[21]{0:T(256)(128)(2,1)S(1)}, u32[]{:S(2)}) copy-start(bf16[21]{0:T(256)(128)(2,1)S(1)} %get-tuple-element.61) | copy-start | bytes 130
  11.5 75.8 %copy-start.83 = (bf16[21]{0:T(256)(128)(2,1)}, bf16[21]{0:T(256)(128)(2,1)S(1)}, u32[]{:S(2)}) copy-start(bf16[21]{0:T(256)(128)(2,1)S(1)} %get-tuple-element.62) | copy-start | bytes 130
  89.3 5.9 copy-start.11
  90.3 38.5 %copy-start.44 = (s32[12288]{0:T(1024)}, s32[12288]{0:T(1024)S(1)}, u32[]{:S(2)}) copy-start(s32[12288]{0:T(1024)S(1)} %reshape.205) | copy-start | bytes 147460
  90.7 4.5 copy-start.55
  91.5 48.5 %copy-start.52 = (s32[4320]{0:T(1024)}, s32[4320]{0:T(1024)S(1)}, u32[]{:S(2)}) copy-start(s32[4320]{0:T(1024)S(1)} %reshape.213) | copy-start | bytes 51844
  128.0 4.0 copy-start.2
  128.2 3.8 copy-start.50
  128.8 116.9 %copy-start.72 = (f32[1,512]{1,0:T(1,128)}, f32[1,512]{1,0:T(1,128)S(1)}, u32[]{:S(2)}) copy-start(f32[1,512]{1,0:T(1,128)S(1)} %get-tuple-element.47) | copy-start | bytes 6148
  128.9 116.9 %copy-start.77 = (f32[1,512]{1,0:T(1,128)}, f32[1,512]{1,0:T(1,128)S(1)}, u32[]{:S(2)}) copy-start(f32[1,512]{1,0:T(1,128)S(1)} %get-tuple-element.48) | copy-start | bytes 6148
  137.5 6.3 collective-permute-start
  137.7 6.1 collective-permute-start.1
  198.1 24.1 %copy-start.31 = (bf16[768,4,128,1]{2,3,1,0:T(2,128)(2,1)S(1)}, bf16[768,4,128,1]{2,3,1,0:T(2,128)(2,1)}, u32[]{:S(2)}) copy-start(bf16[768,4,128,1]{2,3,1,0:T(2,128)(2,1)} %reshape.279) | copy-start | bytes 2359300
  217.7 4.5 copy-start.17
  233.2 8.5 copy-start.38
  245.5 4.3 copy-start.7
  245.5 4.3 copy-start.53
  245.7 4.1 copy-start.60
  245.7 4.1 copy-start.62
  245.8 6.6 copy-start.87
  393.0 380.2 %all-gather.8.cloned.1.call-start = ((), (), s32[]{:S(2)}) async-start(), calls=%async_computation.5 | async-start | bytes 19548160 | tf_op jit(solution)/shard_map/all_gather | solution.py:219
  673.5 735.5 %reduce-scatter.8.cloned.1.call-start = ((), (), s32[]{:S(2)}) async-start(), calls=%async_computation.8 | async-start | bytes 1081344 | tf_op jit(solution)/shard_map/reduce_scatter | solution.py:398
  901.8 9.5 copy-start.23
  903.5 7.8 copy-start.88
  957.9 5.2 copy-start.39
  963.1 4.4 copy-start.22
  1206.0 14.7 copy-start.37
  1206.0 4.4 collective-permute-start.2
  1206.3 6.9 collective-permute-start.3
  1248.3 20.9 %copy-start.71 = (f32[261]{0:T(512)S(1)}, f32[261]{0:T(512)}, u32[]{:S(2)}) copy-start(f32[261]{0:T(512)} %copy-done.70) | copy-start | bytes 3136
  1273.4 277.8 %reduce-scatter.4.cloned.1.call-start = ((), (), s32[]{:S(2)}) async-start(), calls=%async_computation.6 | async-start | bytes 4325376 | tf_op jit(solution)/shard_map/reduce_scatter | solution.py:396
  1280.7 455.4 %reduce-scatter.6.cloned.1.call-start = ((), (), s32[]{:S(2)}) async-start(), calls=%async_computation.7 | async-start | bytes 8650752 | tf_op jit(solution)/shard_map/reduce_scatter | solution.py:397
  1282.1 4.1 copy-start.24
  1295.2 485.6 %copy-start.49 = (f32[64,512]{1,0:T(8,128)S(1)}, f32[64,512]{1,0:T(8,128)}, u32[]{:S(2)}) copy-start(f32[64,512]{1,0:T(8,128)} %param.31) | copy-start | bytes 393220
  1295.2 487.5 %copy-start.42 = (f32[128,512]{1,0:T(8,128)S(1)}, f32[128,512]{1,0:T(8,128)}, u32[]{:S(2)}) copy-start(f32[128,512]{1,0:T(8,128)} %param.32) | copy-start | bytes 786436
  1295.2 632.4 %all-reduce.6.cloned.1.call-start = ((), (), s32[]{:S(2)}) async-start(), calls=%async_computation.9 | async-start | bytes 8388608 | tf_op jit(solution)/shard_map/psum | solution.py:412
  1736.1 46.7 %copy-start.36 = (f32[128,512]{1,0:T(8,128)S(1)}, f32[128,512]{1,0:T(8,128)}, u32[]{:S(2)}) copy-start(f32[128,512]{1,0:T(8,128)} %reduce-scatter.6.cloned.1.call-done) | copy-start | bytes 786436
  1781.7 194.2 %copy-start.30 = (f32[64,512]{1,0:T(8,128)}, f32[64,512]{1,0:T(8,128)S(1)}, u32[]{:S(2)}) copy-start(f32[64,512]{1,0:T(8,128)S(1)} %multiply_add_fusion.3) | copy-start | bytes 393220
  1782.8 189.6 %copy-start.26 = (f32[128,512]{1,0:T(8,128)}, f32[128,512]{1,0:T(8,128)S(1)}, u32[]{:S(2)}) copy-start(f32[128,512]{1,0:T(8,128)S(1)} %multiply_add_fusion.1) | copy-start | bytes 786436
  1943.3 4.5 copy-start.25
  1972.5 4.9 copy-start.1
  (59 other events, 135.2 us)
Sparse Core Ops, SparseCore 0:
  11.6 59.9 all-gather.3
  75.2 61.4 all-gather.5
  393.2 267.7 all-reduce.7
  673.6 99.5 all-gather.7
  1273.5 135.4 reduce-scatter.7
  1411.1 139.9 reduce-scatter.3
  1553.4 182.5 reduce-scatter.5
  1786.5 140.9 all-reduce.5
where the time goes:
time: 2000 us; the launch traced here: 1990 us
  waiting for transfers between devices  922 us (46%)
  local copies, waits for them, and re-layouts  417 us (21%)
  other arithmetic  328 us (16%)
  matrix products  178 us (9%)
  blocking collectives  114 us (6%)
  between operations  23.6 us (1%)
    unnamed x9, waiting for transfers between devices  266 us
    reduce_scatter x1, waiting for transfers between devices, on_device(): lax.psum_scatter(local_grads[1], ('node', 'zero'), scatter_dimension=0, t...  183 us
    reduce_scatter x1, waiting for transfers between devices, on_device(): lax.psum_scatter(local_grads[0], ('node', 'zero'), scatter_dimension=0, t...  141 us
    psum x1, waiting for transfers between devices, on_device(): lax.psum(slotted(gram_of(moment_attn, moment_attn), gram_of(moment_mlp, m...  140 us
    reduce_scatter x1, waiting for transfers between devices, on_device(): lax.psum_scatter(local_grads[2], ('node', 'zero'), scatter_dimension=0, t...  113 us
    scatter-add x1, other arithmetic, backward(): jnp.zeros((rows + 2 * halo_rows, 2 * width), jnp.float32).at[neighbours]  108 us
    unnamed x195, local copies, waits for them, and re-layouts  101 us
    all_gather x1, blocking collectives, on_device(): lax.all_gather(lowered[2], ('node', 'zero'), axis=0, tiled=True)  73.3 us
  transfers between devices with their start and end apart: 12, of which 8 were waited for; matrix products, arithmetic and copies ran while one was open for 10% of the time, Pallas kernels for 0%

commit v1 on v0

v1 whole, which is shorter than its diff:
```python
import math

import jax
import jax.numpy as jnp
import numpy as np
from jax import lax
from jax.sharding import PartitionSpec as P

HEAD_COUNT = 4
NOISE_FEATS = 42
LEVELS = 16
NS_ITERS = 3
STEP = 10

top_precision = lax.Precision.HIGHEST
mid_precision = lax.Precision.HIGH
norm_epsilon = 1e-05
trace_epsilon = 1e-12
clip_limit = 1.0
moment_decay = 0.95
orthogonal_rate = 0.1
adam_first = 0.9
adam_second = 0.95
adam_rate = 0.02
adam_epsilon = 1e-08
average_decay = 0.9
newton_first = 3.4445
newton_second = -4.775
newton_third = 2.0315
sigma_lowest = 0.1
sigma_highest = 20.0
f32 = jnp.float32
bf16 = jnp.bfloat16


def noise_scalars(level):
    sigma = sigma_lowest * (sigma_highest / sigma_lowest) ** (level.astype(f32) / (LEVELS - 1))
    total = sigma * sigma + 1.0
    return (sigma, lax.rsqrt(total), 1.0 / total, sigma * lax.rsqrt(total), total / (sigma * sigma))


def noise_features(sigma):
    half_count = NOISE_FEATS // 2
    frequency = jnp.exp(jnp.arange(half_count).astype(f32) * (3.0 / half_count))
    phases = 0.25 * jnp.log(sigma) * frequency
    return jnp.concatenate([jnp.sin(phases), jnp.cos(phases)])


def normed(rows):
    centred = rows - jnp.mean(rows, axis=-1, keepdims=True)
    spread = jnp.mean(centred * centred, axis=-1, keepdims=True)
    inverse = lax.rsqrt(spread + norm_epsilon)
    return centred * inverse, inverse


def normed_back(grad, unit, inverse, gain):
    scaled = grad * (1.0 + gain)
    back = inverse * (
        scaled
        - jnp.mean(scaled, axis=-1, keepdims=True)
        - unit * jnp.mean(scaled * unit, axis=-1, keepdims=True)
    )
    return back, jnp.sum(grad * unit, axis=0), jnp.sum(grad, axis=0)


def dot(left, right, contract):
    return lax.dot_general(left, right, (contract, ((), ())), preferred_element_type=f32)


def dot_nn(left, right):
    return dot(left, right, ((1,), (0,)))


def dot_nt(left, right):
    return dot(left, right, ((1,), (1,)))


def dot_tn(left, right):
    return dot(left, right, ((0,), (0,)))


def split(value):
    high = value.astype(bf16)
    return high, (value - high.astype(f32)).astype(bf16)


def counted(index, size):
    hits = index[:, :, None] == jnp.arange(size, dtype=index.dtype)
    return jnp.sum(hits.astype(f32), axis=1)


def passed_along(value, axis, steps):
    count = lax.axis_size(axis)
    pairs = [(source, (source + steps) % count) for source in range(count)]
    return lax.ppermute(value, axis, pairs)


def turn_tables(lon_count, modes):
    turns = np.arange(lon_count)[:, None] * np.arange(modes)[None, :] % lon_count
    phases = turns * (2.0 * np.pi / lon_count)
    return np.cos(phases).astype(np.float32), -np.sin(phases).astype(np.float32)


def heads_of(rows):
    return [rows[:, i * 128 : (i + 1) * 128] for i in range(HEAD_COUNT)]


def ns_apply(gram_matrix, moment):
    score_scale = lax.rsqrt(jnp.trace(gram_matrix) + trace_epsilon)
    current = gram_matrix * (score_scale * score_scale)
    identity = jnp.eye(gram_matrix.shape[0], dtype=f32)
    result = moment * score_scale
    for iteration in range(NS_ITERS):
        squared = jnp.dot(current, current, precision=mid_precision)
        polynomial = newton_first * identity + newton_second * current + newton_third * squared
        result = jnp.dot(result, polynomial, precision=mid_precision)
        if iteration + 1 < NS_ITERS:
            current = jnp.dot(
                jnp.dot(polynomial, current, precision=mid_precision),
                polynomial,
                precision=mid_precision,
            )
    return result


def gram_of(left):
    return jnp.dot(left.T, left, precision=mid_precision)


def on_device(
    grid_in,
    target,
    noise_level,
    land_mask,
    neighbours,
    halo_send,
    g2m,
    m2g,
    legendre,
    w_attn,
    w_mlp,
    w_small,
    mom_attn,
    mom_mlp,
    m_small,
    v_small,
    ema_attn,
    ema_mlp,
    ema_small,
):
    cin = grid_in.shape[-1]
    lat_rows, lon_count, channels = target.shape[1:]
    modes, degrees = legendre.shape[1:]
    rows = neighbours.shape[0]
    halo_rows = halo_send.shape[0]
    pixels = m2g.shape[0]
    width = w_attn.shape[1]
    both = ("node", "zero")

    attn_full = lax.all_gather(w_attn.astype(bf16), both, axis=0, tiled=True)
    mlp_full = lax.all_gather(w_mlp.astype(bf16), both, axis=0, tiled=True)
    small_full = lax.all_gather(w_small.astype(bf16), both, axis=0, tiled=True)
    half = mlp_full.shape[0] // 2
    w_query, w_output = attn_full[: 3 * width], attn_full[3 * width :]
    w_upper, w_down = mlp_full[:half], mlp_full[half:]
    w_enc = small_full[:cin]
    w_dec = small_full[cin : cin + channels]
    w_cond = small_full[cin + channels :].reshape(4, -1, width)

    enc_count = (counted(g2m, pixels) * (1.0 / g2m.shape[1])).astype(bf16)
    dec_count = counted(m2g, rows).astype(bf16)
    near_count = counted(neighbours, rows + 2 * halo_rows)
    near_low = near_count.astype(bf16)
    lend = (halo_send[:, None] == jnp.arange(rows, dtype=halo_send.dtype)).astype(bf16)

    sigma, c_input, c_skip, c_output, loss_weight = noise_scalars(noise_level[0])
    scale_input = jnp.where(jnp.arange(cin) < channels, c_input, 1.0)
    inputs = (grid_in[0].reshape(-1, cin).astype(f32) * scale_input).astype(bf16)
    mixed_high, mixed_low = split(dot_nn(enc_count, inputs))
    stream_in = dot_nn(mixed_high, w_enc) + dot_nn(mixed_low, w_enc)
    features = noise_features(sigma).astype(bf16)
    modulation = jnp.einsum("f,jfd->jd", features, w_cond, preferred_element_type=f32)

    unit_one, inverse_one = normed(stream_in)
    first = (unit_one * (1.0 + modulation[0]) + modulation[1]).astype(bf16)
    packed = dot_nt(first, w_query).astype(bf16)
    queries, pairs = packed[:, :width], packed[:, width:]
    lent = dot_nn(lend, pairs).astype(bf16)
    extended = jnp.concatenate(
        [pairs, passed_along(lent, "node", 1), passed_along(lent, "node", -1)], axis=0
    )
    keys, values = heads_of(extended[:, :width]), heads_of(extended[:, width:])
    query_heads = heads_of(queries)
    score_scale = query_heads[0].shape[-1] ** (-0.5)
    present = near_count > 0.0
    probs, probs_low, blended = [], [], []
    for head in range(HEAD_COUNT):
        logits = jnp.where(present, dot_nt(query_heads[head], keys[head]) * score_scale, -jnp.inf)
        raised = jnp.exp(logits - jnp.max(logits, axis=-1, keepdims=True))
        prob = raised / jnp.sum(raised * near_count, axis=-1, keepdims=True)
        low = (prob.astype(bf16).astype(f32) * near_count).astype(bf16)
        probs.append(prob)
        probs_low.append(low)
        blended.append(dot_nn(low, values[head]))
    blended = jnp.concatenate(blended, axis=1).astype(bf16)
    stream_mid = stream_in + dot_nt(blended, w_output)

    unit_two, inverse_two = normed(stream_mid)
    second = (unit_two * (1.0 + modulation[2]) + modulation[3]).astype(bf16)
    upper = dot_nt(second, w_upper)
    activ = jax.nn.gelu(upper).astype(bf16)
    stream_out = stream_mid + dot_nn(activ, w_down)

    out_high, out_low = split(stream_out)
    node_high, node_low = split(dot_nt(out_high, w_dec) + dot_nt(out_low, w_dec))
    third = 1.0 / m2g.shape[1]
    network = (dot_nn(dec_count, node_high) + dot_nn(dec_count, node_low)) * third

    keep_mask = 1.0 - land_mask.astype(f32)[:, :, None] * (
        jnp.arange(channels) == channels - 1
    ).astype(f32)
    predicted = c_skip * grid_in[0, :, :, :channels].astype(f32) + c_output * network.reshape(
        lat_rows, lon_count, channels
    )
    error = (predicted - target[0]) * keep_mask
    cosine, sine = turn_tables(lon_count, modes)
    tables = jnp.stack([jnp.asarray(cosine), jnp.asarray(sine)])
    parts = jnp.einsum("tnc,rnm->rtcm", error, tables, precision=mid_precision)
    weight = loss_weight / (2 * modes * degrees * channels)
    all_parts = lax.all_gather(parts.astype(bf16), "node", axis=1, tiled=True)
    all_legendre = lax.all_gather(legendre, "node", axis=0, tiled=True)
    kernel = jnp.einsum("tml,uml->tum", legendre, all_legendre, precision=top_precision)
    grad_parts = jnp.sum(kernel[None, :, :, None, :] * all_parts[:, None].astype(f32), axis=2)
    loss_here = weight * jnp.sum(grad_parts * parts)
    grad_error = jnp.einsum(
        "rtcm,rnm->tnc", grad_parts * (2.0 * weight), tables, precision=mid_precision
    )
    grad_network = (
        (grad_error * keep_mask * c_output).reshape(lat_rows * lon_count, channels).astype(bf16)
    )

    grad_nodes = dot_tn(dec_count, grad_network) * third
    grad_nodes_high, grad_nodes_low = split(grad_nodes)
    g_dec = dot_tn(grad_nodes_high, out_high)
    grad_out = dot_nn(grad_nodes_high, w_dec) + dot_nn(grad_nodes_low, w_dec)
    grad_branch = grad_out.astype(bf16)
    g_down = dot_tn(activ, grad_branch)
    grad_activ = dot_nt(grad_branch, w_down)
    gelu_value, gelu_back = jax.vjp(jax.nn.gelu, upper)
    grad_upper = gelu_back(grad_activ)[0].astype(bf16)
    g_upper = dot_tn(grad_upper, second)
    grad_second = dot_nn(grad_upper, w_upper)
    back_two, gain_two, bias_two = normed_back(grad_second, unit_two, inverse_two, modulation[2])
    grad_mid = grad_out + back_two
    grad_attn = grad_mid.astype(bf16)
    g_output = dot_tn(grad_attn, blended)
    grad_blended = heads_of(dot_nn(grad_attn, w_output).astype(bf16))
    grad_q, grad_k, grad_v = [], [], []
    for head in range(HEAD_COUNT):
        grad_prob = dot_nt(grad_blended[head], values[head])
        prob = probs[head]
        mean = jnp.sum(prob * near_count * grad_prob, axis=-1, keepdims=True)
        grad_logit = (prob * (grad_prob - mean)).astype(bf16).astype(f32)
        grad_logit = (grad_logit * near_count).astype(bf16)
        grad_q.append(dot_nn(grad_logit, keys[head]) * score_scale)
        grad_k.append(dot_tn(grad_logit, query_heads[head]) * score_scale)
        grad_v.append(dot_tn(probs_low[head], grad_blended[head]))
    grad_queries = jnp.concatenate(grad_q, axis=1)
    grad_extended = jnp.concatenate(grad_k + grad_v, axis=1)
    from_upper = passed_along(grad_extended[rows : rows + halo_rows].astype(bf16), "node", -1)
    from_lower = passed_along(grad_extended[rows + halo_rows :].astype(bf16), "node", 1)
    grad_pairs = grad_extended[:rows] + dot_tn(lend, from_upper) + dot_tn(lend, from_lower)
    grad_packed = jnp.concatenate([grad_queries, grad_pairs], axis=-1).astype(bf16)
    g_query = dot_tn(grad_packed, first)
    grad_first = dot_nn(grad_packed, w_query)
    back_one, gain_one, bias_one = normed_back(grad_first, unit_one, inverse_one, modulation[0])
    grad_in = (grad_mid + back_one).astype(bf16)
    grad_modulation = jnp.stack([gain_one, bias_one, gain_two, bias_two])
    g_cond = jnp.einsum("f,jd->jfd", features.astype(f32), grad_modulation).reshape(-1, width)
    g_enc = dot_tn(mixed_high, grad_in) + dot_tn(mixed_low, grad_in)

    local = (
        jnp.concatenate([g_query, g_output], axis=0),
        jnp.concatenate([g_upper, g_down], axis=0),
        jnp.concatenate([g_enc, g_dec, g_cond], axis=0),
    )
    g_attn, g_mlp = [
        lax.psum_scatter(item.astype(bf16), both, scatter_dimension=0, tiled=True).astype(f32)
        for item in local[:2]
    ]
    g_small = lax.psum_scatter(local[2], both, scatter_dimension=0, tiled=True)

    squares = jnp.sum(g_attn * g_attn) + jnp.sum(g_mlp * g_mlp) + jnp.sum(g_small * g_small)
    total_sq, loss = lax.psum((squares, loss_here), both)
    clip_norm = jnp.sqrt(total_sq)
    factor = jnp.minimum(1.0, clip_limit / clip_norm)
    moment_attn = moment_decay * mom_attn + factor * g_attn
    moment_mlp = moment_decay * mom_mlp + factor * g_mlp

    flat_index = lax.axis_index(both)
    full_rows = lax.axis_size(both)
    attn_upper = (flat_index * w_attn.shape[0] >= 3 * width).astype(f32)
    mlp_upper = (flat_index * w_mlp.shape[0] >= half).astype(f32)
    attn_all = lax.all_gather(moment_attn.astype(bf16), both, axis=0, tiled=True)
    mlp_all = lax.all_gather(moment_mlp.astype(bf16), both, axis=0, tiled=True)
    gram_attn = jnp.where(
        attn_upper > 0.5,
        dot_tn(attn_all[3 * width :], attn_all[3 * width :]),
        dot_tn(attn_all[: 3 * width], attn_all[: 3 * width]),
    )
    mlp_mine = jnp.where(mlp_upper > 0.5, mlp_all[half:], mlp_all[:half])
    gram_mlp = dot_tn(mlp_mine, mlp_mine)
    attn_factor = jnp.where(attn_upper > 0.5, 0.2 * math.sqrt(width), 0.2 * math.sqrt(3 * width))
    mlp_factor = 0.2 * math.sqrt(max(half, width))
    new_attn = w_attn - orthogonal_rate * attn_factor * ns_apply(gram_attn, moment_attn)
    new_mlp = w_mlp - orthogonal_rate * mlp_factor * ns_apply(gram_mlp, moment_mlp)
    clipped = factor * g_small
    first_small = adam_first * m_small + (1.0 - adam_first) * clipped
    second_small = adam_second * v_small + (1.0 - adam_second) * clipped * clipped
    new_small = w_small - adam_rate * (first_small / (1.0 - adam_first**STEP)) / (
        jnp.sqrt(second_small / (1.0 - adam_second**STEP)) + adam_epsilon
    )
    return (
        loss,
        clip_norm,
        new_attn,
        new_mlp,
        new_small,
        moment_attn,
        moment_mlp,
        first_small,
        second_small,
        average_decay * ema_attn + (1.0 - average_decay) * new_attn,
        average_decay * ema_mlp + (1.0 - average_decay) * new_mlp,
        average_decay * ema_small + (1.0 - average_decay) * new_small,
    )


def solution(mesh):
    split_rows = P(("node", "zero"), None)
    return jax.shard_map(
        on_device,
        mesh=mesh,
        in_specs=(
            P("zero", "node", None, None),
            P("zero", "node", None, None),
            P("zero"),
            P("node", None),
            P("node", None),
            P("node"),
            P("node", None),
            P("node", None),
            P("node", None, None),
        )
        + (split_rows,) * 10,
        out_specs=(P(), P()) + (split_rows,) * 10,
        check_vma=False,
    )
```

time: 2000 us -> 895 us (0.45)
  waiting for transfers between devices: 922 us -> 523 us
  local copies, waits for them, and re-layouts: 417 us -> 30 us
  other arithmetic: 328 us -> 61.3 us
  matrix products: 178 us -> 128 us
    unnamed x9 -> x8, waiting for transfers between devices: 266 us -> 0.13 us
    scatter-add x4 -> x0, other arithmetic: 163 us -> none  [the longest x1 108 us: backward(): jnp.zeros((rows + 2 * halo_rows, 2 * width), jnp.float32).at[neighbours]]
    psum x1 -> x0, waiting for transfers between devices: 140 us -> none  [on_device(): lax.psum(slotted(gram_of(moment_attn, moment_attn), gram_of(moment_mlp, m...]
    gather x6 -> x0, local copies, waits for them, and re-layouts: 105 us -> none  [the longest x1 52.7 us: forward(): picked = extended[neighbours]]
    unnamed x195 -> x249, local copies, waits for them, and re-layouts: 101 us -> 16.3 us
    reshape x7 -> x2, local copies, waits for them, and re-layouts: 81 us -> 0.82 us  [the longest x1 0.76 us: on_device(): jnp.einsum('f,jd->jfd', features.astype(f32), grad_modulation)]
    all_gather x3 -> x5, waiting for transfers between devices: 73.2 us -> 130 us  [the longest x1 53.9 us: on_device(): lax.all_gather(moment_attn.astype(bf16), both, axis=0, tiled=True)]
    dot_general x51 -> x79, matrix products: 178 us -> 128 us  [the longest x55 99.4 us: dot(): lax.dot_general(left, right, (contract, ((), ())), preferred_element_type...]
  transfers between devices with their start and end apart: 12 -> 12, of which waited for: 8 -> 7; matrix products, arithmetic and copies ran while one was open for 10% -> 10% of each run, Pallas kernels for 0% -> 0%
where the time goes in v1:
time: 895 us; the launch traced here: 891 us
  waiting for transfers between devices  523 us (58%)
  matrix products  128 us (14%)
  blocking collectives  123 us (14%)
  other arithmetic  61.3 us (7%)
  local copies, waits for them, and re-layouts  30 us (3%)
  between operations  23.1 us (3%)
    reduce_scatter x2, waiting for transfers between devices, on_device(): lax.psum_scatter(item.astype(bf16), both, scatter_dimension=0, tiled=True)  276 us
    reduce_scatter x1, waiting for transfers between devices, on_device(): g_small = lax.psum_scatter(local[2], both, scatter_dimension=0, tiled=True)  114 us
    dot_general x55, matrix products, dot(): lax.dot_general(left, right, (contract, ((), ())), preferred_element_type...  99.4 us
    all_gather x1, blocking collectives, on_device(): small_full = lax.all_gather(w_small.astype(bf16), both, axis=0, tiled=True)  73.9 us
    all_gather x1, waiting for transfers between devices, on_device(): lax.all_gather(moment_attn.astype(bf16), both, axis=0, tiled=True)  53.9 us
    all_gather x1, waiting for transfers between devices, on_device(): mlp_all = lax.all_gather(moment_mlp.astype(bf16), both, axis=0, tiled=True)  49.2 us
    psum x1, blocking collectives, on_device(): total_sq, loss = lax.psum((squares, loss_here), both)  36.9 us
    all_gather x1, waiting for transfers between devices, on_device(): mlp_full = lax.all_gather(w_mlp.astype(bf16), both, axis=0, tiled=True)  26.4 us
  transfers between devices with their start and end apart: 12, of which 7 were waited for; matrix products, arithmetic and copies ran while one was open for 10% of the time, Pallas kernels for 0%

profile of v1, /device:TPU:0, one launch (start us, length us, event | category | flops | bytes accessed | tf_op | source)
XLA Modules:
  0.0 891.3 jit_solution(12267295028151416605)
XLA Ops:
  8.9 2.2 copy.135
  15.8 73.9 %all_gather.22 = bf16[512,512]{1,0:T(8,128)(2,1)S(1)} all-gather(bf16[16,512]{1,0:T(8,128)(2,1)S(1)} %convert_element_type.244), channel_id=1, replica_groups=mesh['node'=4,'zero'=8] {'node','zero'}, dimensions={0}, use_global_device_ids=true | all-gather | bytes 540672 | tf_op jit(solution)/shard_map/all_gather | solution.py:162
  91.2 3.8 convert_reduce_fusion.2
  95.0 2.9 convert_reduce_fusion.1
  101.2 6.1 convert_reduce_fusion
  108.7 4.0 convolution_convert_fusion
  115.9 6.2 fusion.50
  128.7 2.1 multiply_reduce_fusion.8
  131.0 2.7 multiply_convert_fusion.13
  140.4 26.4 %all-gather.10.cloned.1.call-done = bf16[4096,512]{1,0:T(8,128)(2,1)} async-done(((bf16[128,512]{1,0:T(8,128)(2,1)}), bf16[4096,512]{1,0:T(8,128)(2,1)}) %all-gather.10.cloned.1.call-update) | async-done | bytes 4194320 | tf_op jit(solution)/shard_map/all_gather | solution.py:161
  166.8 4.3 fusion.26
  171.1 2.9 fusion.31
  179.0 3.1 fusion.190
  182.5 12.0 %all_gather.25 = bf16[2,16,83,181]{3,0,2,1:T(2,128)(2,1)S(1)} all-gather(bf16[2,4,83,181]{3,0,2,1:T(2,128)(2,1)S(1)} %copy.142), channel_id=1, replica_groups=mesh['node'=4,'zero'=8] {'node'}, dimensions={1}, use_global_device_ids=true | all-gather | bytes 1201840 | tf_op jit(solution)/shard_map/all_gather | solution.py:230
  194.9 3.0 multiply_reduce_fusion
  199.9 2.1 convolution_multiply_fusion.14
  204.8 8.0 fusion.6
  212.9 3.0 fusion.191
  215.9 3.1 copy.148
  219.0 2.6 multiply_reduce_fusion.9
  221.8 2.0 multiply_add_fusion
  223.8 2.2 convolution_convert_fusion.4
  230.1 4.3 multiply_reduce_fusion.1
  234.4 5.5 multiply_convert_fusion.2
  239.9 3.0 fusion.53
  242.9 2.8 fusion.46
  245.7 1.9 multiply_convert_fusion.6
  248.7 2.6 fusion.55
  254.5 2.9 fusion.45
  257.4 2.9 fusion.44
  267.2 2.4 convert.63
  272.7 3.2 collective-permute-done.2
  278.2 2.6 fusion.192
  280.8 2.0 copy.153
  285.4 2.0 add_convert_fusion
  289.9 1.9 convolution_convert_fusion.5
  295.6 3.9 convolution_convert_fusion.2
  299.5 5.6 convolution_convert_fusion.1
  305.1 2.2 pad_maximum_fusion
  310.1 113.7 %reduce-scatter.8.cloned.1.call-done = f32[16,512]{1,0:T(8,128)} async-done(((f32[512,512]{1,0:T(8,128)}), f32[16,512]{1,0:T(8,128)}) %reduce-scatter.8.cloned.1.call-update) | async-done | bytes 32784 | tf_op jit(solution)/shard_map/reduce_scatter | solution.py:291
  425.2 134.6 %reduce-scatter.4.cloned.1.call-done = bf16[64,512]{1,0:T(8,128)(2,1)} async-done(((bf16[2048,512]{1,0:T(8,128)(2,1)}), bf16[64,512]{1,0:T(8,128)(2,1)}) %reduce-scatter.4.cloned.1.call-update) | async-done | bytes 65552 | tf_op jit(solution)/shard_map/reduce_scatter | solution.py:288
  561.2 141.5 %reduce-scatter.6.cloned.1.call-done = bf16[128,512]{1,0:T(8,128)(2,1)} async-done(((bf16[4096,512]{1,0:T(8,128)(2,1)}), bf16[128,512]{1,0:T(8,128)(2,1)}) %reduce-scatter.6.cloned.1.call-update) | async-done | bytes 131088 | tf_op jit(solution)/shard_map/reduce_scatter | solution.py:288
  706.3 36.9 %all-reduce = (f32[]{:T(128)}, f32[]{:T(128)}) all-reduce(f32[]{:T(128)S(6)} %mul.631, f32[]{:T(128)S(6)} %add.208), channel_id=1, replica_groups=mesh['node'=4,'zero'=8] {'node','zero'}, use_global_device_ids=true, to_apply=%region_17.18 | all-reduce | flops 2 | bytes 16 | tf_op jit(solution)/shard_map/psum | solution.py:294
  748.8 53.9 %all-gather.12.cloned.1.call-done = bf16[2048,512]{1,0:T(8,128)(2,1)} async-done(((bf16[64,512]{1,0:T(8,128)(2,1)}), bf16[2048,512]{1,0:T(8,128)(2,1)}) %all-gather.12.cloned.1.call-update) | async-done | bytes 2097168 | tf_op jit(solution)/shard_map/all_gather | solution.py:304
  802.8 3.0 fusion.29
  805.7 2.3 select_reduce_fusion.1
  818.1 49.2 %all-gather.14.cloned.1.call-done = bf16[4096,512]{1,0:T(8,128)(2,1)} async-done(((bf16[128,512]{1,0:T(8,128)(2,1)}), bf16[4096,512]{1,0:T(8,128)(2,1)}) %all-gather.14.cloned.1.call-update) | async-done | bytes 4194320 | tf_op jit(solution)/shard_map/all_gather | solution.py:305
  867.3 5.4 select_reduce_fusion
  (382 shorter events, 97.5 us)
Async XLA Ops:
  7.2 6.2 copy-start.49
  7.2 101.5 %all-gather.8.cloned.1.call-start = ((), (), s32[]{:S(2)}) async-start(), calls=%async_computation.4 | async-start | bytes 2162688 | tf_op jit(solution)/shard_map/all_gather | solution.py:160
  8.9 107.0 %all-gather.6.cloned.1.call-start = ((), (), s32[]{:S(2)}) async-start(), calls=%async_computation.3 | async-start | bytes 3768320 | tf_op jit(solution)/shard_map/all_gather | solution.py:231
  11.2 4.6 copy-start.61
  11.2 155.6 %all-gather.10.cloned.1.call-start = ((), (), s32[]{:S(2)}) async-start(), calls=%async_computation.5 | async-start | bytes 4325376 | tf_op jit(solution)/shard_map/all_gather | solution.py:161
  11.9 79.3 %copy-start.93 = (s32[1440,3]{0,1:T(4,128)S(1)}, s32[1440,3]{0,1:T(4,128)}, u32[]{:S(2)}) copy-start(s32[1440,3]{0,1:T(4,128)} %param.28) | copy-start | bytes 51844
  12.0 411.8 %reduce-scatter.8.cloned.1.call-start = ((), (), s32[]{:S(2)}) async-start(), calls=%async_computation.8 | async-start | bytes 1081344 | tf_op jit(solution)/shard_map/reduce_scatter | solution.py:291
  15.1 79.9 %copy-start.103 = (s32[768,4]{0,1:T(4,128)S(1)}, s32[768,4]{0,1:T(4,128)}, u32[]{:S(2)}) copy-start(s32[768,4]{0,1:T(4,128)} %param.27) | copy-start | bytes 36868
  89.7 84.6 %copy-start.45 = (bf16[512,512]{1,0:T(8,128)(2,1)}, bf16[512,512]{1,0:T(8,128)(2,1)S(1)}, u32[]{:S(2)}) copy-start(bf16[512,512]{1,0:T(8,128)(2,1)S(1)} %all_gather.22) | copy-start | bytes 1572868
  91.2 17.4 %copy-start.95 = (f32[1,512]{1,0:T(1,128)}, f32[1,512]{1,0:T(1,128)S(1)}, u32[]{:S(2)}) copy-start(f32[1,512]{1,0:T(1,128)S(1)} %get-tuple-element.48) | copy-start | bytes 6148
  91.2 17.4 %copy-start.106 = (f32[1,512]{1,0:T(1,128)}, f32[1,512]{1,0:T(1,128)S(1)}, u32[]{:S(2)}) copy-start(f32[1,512]{1,0:T(1,128)S(1)} %get-tuple-element.47) | copy-start | bytes 6148
  100.1 8.6 copy-start.67
  101.2 7.4 copy-start.80
  108.7 5.6 copy-start.108
  115.3 7.9 collective-permute-start.1
  115.3 7.9 collective-permute-start
  125.9 10.0 %copy-start.25 = (bf16[960,1024]{1,0:T(8,128)(2,1)}, bf16[960,1024]{1,0:T(8,128)(2,1)S(1)}, u32[]{:S(2)}) copy-start(bf16[960,1024]{1,0:T(8,128)(2,1)S(1)} %pad_maximum_fusion.2) | copy-start | bytes 5898244
  126.6 4.3 copy-start.3
  126.6 4.3 copy-start.71
  134.7 4.3 copy-start.117
  137.3 29.5 %copy-start.98 = (f32[1,512]{1,0:T(1,128)S(1)}, f32[1,512]{1,0:T(1,128)}, u32[]{:S(2)}) copy-start(f32[1,512]{1,0:T(1,128)} %get-tuple-element.45) | copy-start | bytes 6148
  139.0 32.0 %copy-start.69 = (f32[768]{0:T(1024)}, f32[768]{0:T(1024)S(1)}, u32[]{:S(2)}) copy-start(f32[768]{0:T(1024)S(1)} %broadcast_multiply_fusion.4) | copy-start | bytes 9220
  140.4 30.7 %copy-start.82 = (f32[768]{0:T(1024)}, f32[768]{0:T(1024)S(1)}, u32[]{:S(2)}) copy-start(f32[768]{0:T(1024)S(1)} %add_rsqrt_fusion) | copy-start | bytes 9220
  166.8 4.3 copy-start.16
  166.8 4.3 copy-start.112
  204.8 8.0 copy-start.27
  234.4 8.5 copy-start.31
  239.9 7.7 copy-start.43
  248.7 5.8 copy-start.32
  254.5 5.8 copy-start.44
  257.4 4.3 copy-start.42
  269.6 6.3 copy-start.109
  269.7 7.0 collective-permute-start.3
  270.1 5.8 collective-permute-start.2
  271.6 5.0 copy-start.24
  289.6 270.1 %reduce-scatter.4.cloned.1.call-start = ((), (), s32[]{:S(2)}) async-start(), calls=%async_computation.6 | async-start | bytes 2162688 | tf_op jit(solution)/shard_map/reduce_scatter | solution.py:288
  294.9 4.6 copy-start.28
  294.9 407.8 %reduce-scatter.6.cloned.1.call-start = ((), (), s32[]{:S(2)}) async-start(), calls=%async_computation.7 | async-start | bytes 4325376 | tf_op jit(solution)/shard_map/reduce_scatter | solution.py:288
  307.4 436.6 %copy-start.63 = (f32[64,512]{1,0:T(8,128)S(1)}, f32[64,512]{1,0:T(8,128)}, u32[]{:S(2)}) copy-start(f32[64,512]{1,0:T(8,128)} %param.33) | copy-start | bytes 393220
  307.4 438.3 %copy-start.58 = (f32[128,512]{1,0:T(8,128)S(1)}, f32[128,512]{1,0:T(8,128)}, u32[]{:S(2)}) copy-start(f32[128,512]{1,0:T(8,128)} %param.34) | copy-start | bytes 786436
  307.4 440.0 %copy-start.62 = (f32[16,512]{1,0:T(8,128)S(1)}, f32[16,512]{1,0:T(8,128)}, u32[]{:S(2)}) copy-start(f32[16,512]{1,0:T(8,128)} %param.32) | copy-start | bytes 98308
  307.4 440.0 %copy-start.90 = (f32[16,512]{1,0:T(8,128)S(1)}, f32[16,512]{1,0:T(8,128)}, u32[]{:S(2)}) copy-start(f32[16,512]{1,0:T(8,128)} %param.39) | copy-start | bytes 98308
  307.4 440.0 %copy-start.91 = (f32[16,512]{1,0:T(8,128)S(1)}, f32[16,512]{1,0:T(8,128)}, u32[]{:S(2)}) copy-start(f32[16,512]{1,0:T(8,128)} %param.35) | copy-start | bytes 98308
  307.4 440.0 %copy-start.92 = (f32[16,512]{1,0:T(8,128)S(1)}, f32[16,512]{1,0:T(8,128)}, u32[]{:S(2)}) copy-start(f32[16,512]{1,0:T(8,128)} %param.36) | copy-start | bytes 98308
  307.4 495.3 %all-gather.12.cloned.1.call-start = ((), (), s32[]{:S(2)}) async-start(), calls=%async_computation.9 | async-start | bytes 2162688 | tf_op jit(solution)/shard_map/all_gather | solution.py:304
  745.4 64.4 %copy-start.56 = (f32[64,512]{1,0:T(8,128)}, f32[64,512]{1,0:T(8,128)S(1)}, u32[]{:S(2)}) copy-start(f32[64,512]{1,0:T(8,128)S(1)} %get-tuple-element.35) | copy-start | bytes 393220
  745.4 121.9 %all-gather.14.cloned.1.call-start = ((), (), s32[]{:S(2)}) async-start(), calls=%async_computation.10 | async-start | bytes 4325376 | tf_op jit(solution)/shard_map/all_gather | solution.py:305
  747.3 129.4 %copy-start.53 = (f32[128,512]{1,0:T(8,128)}, f32[128,512]{1,0:T(8,128)S(1)}, u32[]{:S(2)}) copy-start(f32[128,512]{1,0:T(8,128)S(1)} %get-tuple-element.33) | copy-start | bytes 786436
  (87 other events, 210.9 us)
Sparse Core Ops, SparseCore 0:
  11.6 60.7 all-gather.7
  73.9 26.4 all-gather.5
  104.0 62.7 all-gather.9
  289.7 134.0 reduce-scatter.7
  426.0 133.7 reduce-scatter.3
  561.9 140.8 reduce-scatter.5
  745.6 57.1 all-gather.11
  806.3 60.9 all-gather.13

commit v2 on v1

--- a/solution.py
+++ b/solution.py
@@ -4,6 +4,8 @@
 import jax.numpy as jnp
 import numpy as np
 from jax import lax
+from jax.experimental import pallas as pl
+from jax.experimental.pallas import tpu as pltpu
 from jax.sharding import PartitionSpec as P
 
 HEAD_COUNT = 4
@@ -31,6 +33,526 @@
 sigma_highest = 20.0
 f32 = jnp.float32
 bf16 = jnp.bfloat16
+
+
+MESH = pl.DeviceIdType.MESH
+ROW_CHUNK = 16
+
+
+class Place:
+    def __init__(self, nodes, zeros):
+        self.uppers, self.cores = nodes // 2, 2
+        self.nears = 2 if zeros < 16 else 4
+        self.fars = zeros // self.nears
+        self.mates = max(self.uppers // 2, 1)
+        self.zeros = zeros
+
+    def locate(self):
+        node, zero = lax.axis_index("node"), lax.axis_index("zero")
+        self.upper, self.core = node // 2, node % 2
+        self.far, self.near = zero // self.nears, zero % self.nears
+
+    def moved(self, upper=0, core=0, far=0, near=0, mate=0):
+        row = lax.rem(self.upper + upper, self.uppers) if upper else self.upper
+        if mate:
+            group = self.upper // self.mates * self.mates
+            row = group + lax.rem(self.upper - group + mate, self.mates)
+        return (
+            row,
+            1 - self.core if core else self.core,
+            lax.rem(self.far + far, self.fars) if far else self.far,
+            lax.rem(self.near + near, self.nears) if near else self.near,
+        )
+
+    def device(self, **steps):
+        upper, core, far, near = self.moved(**steps)
+        return (upper * 2 + core, far * self.nears + near)
+
+    def slot(self, upper, core, far, near):
+        return (upper * 2 + core) * self.zeros + far * self.nears + near
+
+    def peers(self):
+        return (
+            [dict(far=k) for k in range(1, self.fars)]
+            + [dict(near=j) for j in range(1, self.nears)]
+            + [dict(upper=i) for i in range(1, self.uppers)]
+            + [dict(core=1)]
+        )
+
+    def greet(self):
+        barrier = pltpu.get_barrier_semaphore()
+        for steps in self.peers():
+            pl.semaphore_signal(barrier, 1, device_id=self.device(**steps), device_id_type=MESH)
+        pl.semaphore_wait(barrier, len(self.peers()))
+
+
+def half_rows(rows):
+    return (rows // 2 + 15) // 16 * 16
+
+
+def gather_body(place, shard, out, own_sem, far_sem, near_sem, upper_sem, over_sem, under_sem, core_sem):
+    rows = shard.shape[0]
+    head = half_rows(rows)
+    parts = (pl.ds(0, head), pl.ds(head, rows - head))
+    fars, nears, uppers = place.fars, place.nears, place.uppers
+    here = place.slot(*place.moved())
+    kept = pltpu.make_async_copy(shard, out.at[here], own_sem)
+    kept.start()
+    started = []
+
+    def send(source, target, sems, **steps):
+        copy = pltpu.make_async_remote_copy(
+            src_ref=source,
+            dst_ref=target,
+            send_sem=sems.at[0],
+            recv_sem=sems.at[1],
+            device_id=place.device(**steps),
+            device_id_type=MESH,
+        )
+        copy.start()
+        started.append(copy)
+        return copy
+
+    def block(upper=0, far=0, near=0):
+        return out.at[place.slot(*place.moved(upper=upper, far=far, near=near))]
+
+    def back(steps, size):
+        return (size - steps) % size
+
+    far_copies = {}
+    for k in range(1, fars):
+        far_copies[k] = send(shard, out.at[here], far_sem.at[k], far=k)
+    near_copies, upper_copies, over, under, cores = {}, {}, {}, {}, []
+
+    def first(k):
+        if k:
+            far_copies[k].wait_recv()
+        target = block(far=back(k, fars))
+        source = target if k else shard
+        for j in range(1, nears):
+            near_copies[k, j] = send(source, target, near_sem.at[k, j], near=j)
+        for i in range(1, uppers):
+            upper_copies[k, i] = send(source, target, upper_sem.at[k, i], upper=i)
+        cores.append(send(source, target, core_sem.at[k, 0, 0], core=1))
+
+    def second(k):
+        for j in range(1, nears):
+            near_copies[k, j].wait_recv()
+            item = block(far=back(k, fars), near=back(j, nears))
+            for i in range(1, uppers):
+                over[k, j, i] = send(
+                    item.at[parts[0]], item.at[parts[0]], over_sem.at[k, j, i], upper=i
+                )
+            cores.append(send(item, item, core_sem.at[k, j, 0], core=1))
+        for i in range(1, uppers):
+            upper_copies[k, i].wait_recv()
+            item = block(far=back(k, fars), upper=back(i, uppers))
+            for j in range(1, nears):
+                under[k, j, i] = send(
+                    item.at[parts[1]], item.at[parts[1]], under_sem.at[k, j, i], near=j
+                )
+            cores.append(send(item, item, core_sem.at[k, 0, i], core=1))
+
+    def third(k):
+        for j in range(1, nears):
+            for i in range(1, uppers):
+                over[k, j, i].wait_recv()
+                under[k, j, i].wait_recv()
+                item = block(far=back(k, fars), near=back(j, nears), upper=back(i, uppers))
+                cores.append(send(item, item, core_sem.at[k, j, i], core=1))
+
+    for k in range(fars + 2):
+        if k < fars:
+            first(k)
+        if 1 <= k <= fars:
+            second(k - 1)
+        if k >= 2:
+            third(k - 2)
+    kept.wait()
+    for copy in cores:
+        copy.wait_recv()
+    for copy in started:
+        copy.wait_send()
+
+
+def gather_sems(place):
+    dma = pltpu.SemaphoreType.DMA
+    fars, nears, uppers = place.fars, place.nears, place.uppers
+    return [
+        dma,
+        dma((fars, 2)),
+        dma((fars, nears, 2)),
+        dma((fars, uppers, 2)),
+        dma((fars, nears, uppers, 2)),
+        dma((fars, nears, uppers, 2)),
+        dma((fars, nears, uppers, 2)),
+    ]
+
+
+def gather_weights(nodes, zeros, w_attn, w_mlp, w_small, collective):
+    place = Place(nodes, zeros)
+    sizes = [w.shape[0] for w in (w_attn, w_mlp, w_small)]
+    rows = -(-sum(sizes) // 16) * 16
+    width = w_attn.shape[1]
+
+    def kernel(attn_ref, mlp_ref, small_ref, out_ref, shard, *sems):
+        place.locate()
+        start = 0
+        for ref, size in zip((attn_ref, mlp_ref, small_ref), sizes):
+            shard[pl.ds(start, size)] = ref[...].astype(bf16)
+            start += size
+        place.greet()
+        gather_body(place, shard, out_ref, *sems)
+
+    return pl.pallas_call(
+        kernel,
+        out_shape=jax.ShapeDtypeStruct((nodes * zeros, rows, width), bf16),
+        in_specs=[pl.BlockSpec(memory_space=pltpu.VMEM)] * 3,
+        out_specs=pl.BlockSpec(memory_space=pl.ANY),
+        scratch_shapes=[pltpu.VMEM((rows, width), bf16)] + gather_sems(place),
+        compiler_params=pltpu.CompilerParams(
+            collective_id=collective, has_side_effects=True, vmem_limit_bytes=48 << 20
+        ),
+    )(w_attn, w_mlp, w_small)
+
+
+def scatter_body(place, grads, own, bufs, sems):
+    (core_in, over_out, over_in, under_out, under_in, over_out2, over_in2, under_out2, under_in2, far_out, far_in) = bufs
+    (core_sem, over_sem, under_sem, over_sem2, under_sem2, far_sem) = sems
+    rows = grads.shape[1]
+    head = half_rows(rows)
+    tail = rows - head
+    fars, nears, uppers = place.fars, place.nears, place.uppers
+    started = []
+
+    def send(source, target, sem, **steps):
+        copy = pltpu.make_async_remote_copy(
+            src_ref=source,
+            dst_ref=target,
+            send_sem=sem.at[0],
+            recv_sem=sem.at[1],
+            device_id=place.device(**steps),
+            device_id_type=MESH,
+        )
+        copy.start()
+        started.append(copy)
+        return copy
+
+    def add(target, sources, count):
+        @pl.loop(0, count // ROW_CHUNK)
+        def _(index):
+            spot = pl.ds(pl.multiple_of(index * ROW_CHUNK, ROW_CHUNK), ROW_CHUNK)
+            total = sources[0][spot].astype(f32)
+            for source in sources[1:]:
+                total += source[spot].astype(f32)
+            target[spot] = total.astype(target.dtype)
+
+    order = list(range(1, fars)) + [0]
+    core_copies = {}
+    other = 1 - place.core
+    for k in order:
+        far = place.moved(far=k)[2]
+        for i in range(uppers):
+            first = place.slot(i, other, far, 0)
+            core_copies[k, i] = send(
+                grads.at[pl.ds(first, nears)], core_in.at[k, i], core_sem.at[k, i], core=1
+            )
+
+    over, under, over2, under2, far_copies = {}, {}, {}, {}, {}
+
+    def pair(k, upper, near, part):
+        far = place.moved(far=k)[2]
+        return [
+            grads.at[place.slot(upper, place.core, far, near), part],
+            core_in.at[k, upper, near, part],
+        ]
+
+    top, low = pl.ds(0, head), pl.ds(head, tail)
+
+    def one(k):
+        for i in range(uppers):
+            core_copies[k, i].wait_recv()
+        for i in range(1, uppers):
+            for near in range(nears):
+                add(over_out.at[k, i, near], pair(k, place.moved(upper=i)[0], near, top), head)
+            over[k, i] = send(over_out.at[k, i], over_in.at[k, i], over_sem.at[k, i], upper=i)
+        for j in range(1, nears):
+            for upper in range(uppers):
+                add(under_out.at[k, j, upper], pair(k, upper, place.moved(near=j)[3], low), tail)
+            under[k, j] = send(under_out.at[k, j], under_in.at[k, j], under_sem.at[k, j], near=j)
+
+    def top_sum(k, near):
+        return pair(k, place.upper, near, top) + [
+            over_in.at[k, i, near] for i in range(1, uppers)
+        ]
+
+    def low_sum(k, upper):
+        return pair(k, upper, place.near, low) + [
+            under_in.at[k, j, upper] for j in range(1, nears)
+        ]
+
+    def two(k):
+        for i in range(1, uppers):
+            over[k, i].wait_recv()
+        for j in range(1, nears):
+            add(over_out2.at[k, j], top_sum(k, place.moved(near=j)[3]), head)
+            over2[k, j] = send(over_out2.at[k, j], over_in2.at[k, j], over_sem2.at[k, j], near=j)
+        for j in range(1, nears):
+            under[k, j].wait_recv()
+        for i in range(1, uppers):
+            add(under_out2.at[k, i], low_sum(k, place.moved(upper=i)[0]), tail)
+            under2[k, i] = send(
+                under_out2.at[k, i], under_in2.at[k, i], under_sem2.at[k, i], upper=i
+            )
+
+    def ready(k):
+        for j in range(1, nears):
+            over2[k, j].wait_recv()
+        for i in range(1, uppers):
+            under2[k, i].wait_recv()
+        return (
+            top_sum(k, place.near) + [over_in2.at[k, j] for j in range(1, nears)],
+            low_sum(k, place.upper) + [under_in2.at[k, i] for i in range(1, uppers)],
+        )
+
+    def three(k):
+        tops, lows = ready(k)
+        add(far_out.at[k, top], tops, head)
+        add(far_out.at[k, low], lows, tail)
+        far_copies[k] = send(far_out.at[k], far_in.at[k], far_sem.at[k], far=k)
+
+    for step in range(fars + 2):
+        if step < fars:
+            one(order[step])
+        if 1 <= step <= fars:
+            two(order[step - 1])
+        if 2 <= step and order[step - 2]:
+            three(order[step - 2])
+    tops, lows = ready(0)
+    for k in range(1, fars):
+        far_copies[k].wait_recv()
+    add(own.at[top], tops + [far_in.at[k, top] for k in range(1, fars)], head)
+    add(own.at[low], lows + [far_in.at[k, low] for k in range(1, fars)], tail)
+    for copy in started:
+        copy.wait_send()
+
+
+def scatter_scratch(place, rows, width):
+    fars, nears, uppers = place.fars, place.nears, place.uppers
+    head = half_rows(rows)
+    tail = rows - head
+    vmem = lambda *shape: pltpu.VMEM(shape + (width,), bf16)
+    dma = pltpu.SemaphoreType.DMA
+    bufs = [vmem(fars, uppers, nears, rows)]
+    bufs += [vmem(fars, uppers, nears, head)] * 2
+    bufs += [vmem(fars, nears, uppers, tail)] * 2
+    bufs += [vmem(fars, nears, head)] * 2
+    bufs += [vmem(fars, uppers, tail)] * 2
+    bufs += [vmem(fars, rows)] * 2
+    sems = [
+        dma((fars, uppers, 2)),
+        dma((fars, uppers, 2)),
+        dma((fars, nears, 2)),
+        dma((fars, nears, 2)),
+        dma((fars, uppers, 2)),
+        dma((fars, 2)),
+    ]
+    return bufs, sems
+
+
+def sixteens(rows):
+    return -(-rows // 16) * 16
+
+
+def moment_gather_body(place, shard, out, low, own_sem, far_sem, near_sem, upper_sem, mate_sem, core_sem):
+    rows = shard.shape[0]
+    fars, nears, uppers, mates = place.fars, place.nears, place.uppers, place.mates
+    base, rest = pl.ds(0, low), pl.ds(low, rows - low)
+    here = place.slot(*place.moved())
+    kept = pltpu.make_async_copy(shard, out.at[here], own_sem)
+    kept.start()
+    started, cores = [], []
+
+    def send(source, target, sems, **steps):
+        copy = pltpu.make_async_remote_copy(
+            src_ref=source,
+            dst_ref=target,
+            send_sem=sems.at[0],
+            recv_sem=sems.at[1],
+            device_id=place.device(**steps),
+            device_id_type=MESH,
+        )
+        copy.start()
+        started.append(copy)
+        return copy
+
+    def block(**steps):
+        return out.at[place.slot(*place.moved(**steps))]
+
+    far_copies, near_copies, upper_copies, mate_copies = {}, {}, {}, {}
+    for k in range(1, fars):
+        far_copies[k] = send(shard, out.at[here], far_sem.at[k], far=k)
+
+    def spread(k, j, source, target):
+        for i in range(1, uppers):
+            upper_copies[k, j, i] = send(
+                source.at[base], target.at[base], upper_sem.at[k, j, i], upper=i
+            )
+        for i in range(1, mates):
+            mate_copies[k, j, i] = send(
+                source.at[rest], target.at[rest], mate_sem.at[k, j, i], mate=i
+            )
+        cores.append(send(source, target, core_sem.at[k, j, 0, 0], core=1))
+
+    def first(k):
+        if k:
+            far_copies[k].wait_recv()
+        target = block(far=(fars - k) % fars)
+        source = target if k else shard
+        for j in range(1, nears):
+            near_copies[k, j] = send(source, target, near_sem.at[k, j], near=j)
+        spread(k, 0, source, target)
+
+    def second(k):
+        for j in range(1, nears):
+            near_copies[k, j].wait_recv()
+            item = block(far=(fars - k) % fars, near=nears - j)
+            spread(k, j, item, item)
+
+    def third(k):
+        for j in range(nears):
+            steps = dict(far=(fars - k) % fars, near=(nears - j) % nears)
+            for i in range(1, uppers):
+                upper_copies[k, j, i].wait_recv()
+                item = block(upper=uppers - i, **steps).at[base]
+                cores.append(send(item, item, core_sem.at[k, j, i, 0], core=1))
+            for i in range(1, mates):
+                mate_copies[k, j, i].wait_recv()
+                item = block(mate=mates - i, **steps).at[rest]
+                cores.append(send(item, item, core_sem.at[k, j, i, 1], core=1))
+
+    for k in range(fars + 2):
+        if k < fars:
+            first(k)
+        if 1 <= k <= fars:
+            second(k - 1)
+        if k >= 2:
+            third(k - 2)
+    kept.wait()
+    for copy in cores:
+        copy.wait_recv()
+    for copy in started:
+        copy.wait_send()
+
+
+def moment_gather_sems(place):
+    dma = pltpu.SemaphoreType.DMA
+    fars, nears, uppers, mates = place.fars, place.nears, place.uppers, place.mates
+    return [
+        dma,
+        dma((fars, 2)),
+        dma((fars, nears, 2)),
+        dma((fars, nears, uppers, 2)),
+        dma((fars, nears, max(mates, 2), 2)),
+        dma((fars, nears, uppers, 2, 2)),
+    ]
+
+
+def total_body(place, tile, slots, sems):
+    value = tile
+    upper, core, far, near = place.moved()
+    stages = (
+        (dict(core=1), 2, core),
+        (dict(near=1), place.nears, near),
+        (dict(upper=1), place.uppers, upper),
+        (dict(far=1), place.fars, far),
+    )
+    for stage, (axis, size, mine) in enumerate(stages):
+        name = list(axis)[0]
+        slots[stage, mine] = value
+        copies = []
+        for step in range(1, size):
+            copy = pltpu.make_async_remote_copy(
+                src_ref=slots.at[stage, mine],
+                dst_ref=slots.at[stage, mine],
+                send_sem=sems.at[stage, step, 0],
+                recv_sem=sems.at[stage, step, 1],
+                device_id=place.device(**{name: step}),
+                device_id_type=MESH,
+            )
+            copy.start()
+            copies.append(copy)
+        for copy in copies:
+            copy.wait()
+        value = slots[stage, 0]
+        for other in range(1, size):
+            value = value + slots[stage, other]
+    return value
+
+
+def reduce_and_gather(nodes, zeros, grads, loss_tile, mom_attn, mom_mlp, small_rows, collective):
+    place = Place(nodes, zeros)
+    devices, rows, width = grads.shape
+    attn_rows, mlp_rows = mom_attn.shape[0], mom_mlp.shape[0]
+    low = sixteens(attn_rows)
+    moment_rows = low + sixteens(mlp_rows)
+    bufs, sems = scatter_scratch(place, rows, width)
+    total_sems = [
+        pltpu.VMEM((4, max(place.fars, place.uppers, place.nears, 2), 8, 128), f32),
+        pltpu.SemaphoreType.DMA((4, max(place.fars, place.uppers, place.nears, 2), 2)),
+    ]
+    moment_sems = moment_gather_sems(place)
+
+    def kernel(
+        grads_ref, loss_ref, attn_ref, mlp_ref, small_out, attn_out, mlp_out, total_out, all_out,
+        own, shard, *scratch,
+    ):
+        place.locate()
+        place.greet()
+        first = len(bufs)
+        second = first + len(sems)
+        scatter_body(place, grads_ref, own, scratch[:first], scratch[first:second])
+        g_attn = own[pl.ds(0, attn_rows)]
+        g_mlp = own[pl.ds(attn_rows, mlp_rows)]
+        start = attn_rows + mlp_rows
+        g_small = own[pl.ds(start, small_rows)] + own[pl.ds(start + small_rows, small_rows)]
+        small_out[...] = g_small
+        squares = jnp.sum(g_attn * g_attn) + jnp.sum(g_mlp * g_mlp) + jnp.sum(g_small * g_small)
+        row = lax.broadcasted_iota(jnp.int32, (8, 128), 0)
+        tile = jnp.where(row < 4, squares, loss_ref[...])
+        slots, slot_sems = scratch[second : second + 2]
+        total = total_body(place, tile, slots, slot_sems)
+        total_out[...] = total
+        factor = jnp.minimum(1.0, clip_limit * lax.rsqrt(total[0:1, 0:1]))
+        new_attn = moment_decay * attn_ref[...] + factor * g_attn
+        new_mlp = moment_decay * mlp_ref[...] + factor * g_mlp
+        attn_out[...] = new_attn
+        mlp_out[...] = new_mlp
+        shard[pl.ds(0, attn_rows)] = new_attn.astype(bf16)
+        shard[pl.ds(low, mlp_rows)] = new_mlp.astype(bf16)
+        moment_gather_body(place, shard, all_out, low, *scratch[second + 2 :])
+
+    vmem = pl.BlockSpec(memory_space=pltpu.VMEM)
+    return pl.pallas_call(
+        kernel,
+        out_shape=(
+            jax.ShapeDtypeStruct((small_rows, width), f32),
+            jax.ShapeDtypeStruct((attn_rows, width), f32),
+            jax.ShapeDtypeStruct((mlp_rows, width), f32),
+            jax.ShapeDtypeStruct((8, 128), f32),
+            jax.ShapeDtypeStruct((devices, moment_rows, width), bf16),
+        ),
+        in_specs=[vmem] * 4,
+        out_specs=(vmem, vmem, vmem, vmem, pl.BlockSpec(memory_space=pl.ANY)),
+        scratch_shapes=[pltpu.VMEM((rows, width), f32), pltpu.VMEM((moment_rows, width), bf16)]
+        + bufs
+        + sems
+        + total_sems
+        + moment_sems,
+        compiler_params=pltpu.CompilerParams(
+            collective_id=collective, has_side_effects=True, vmem_limit_bytes=56 << 20
+        ),
+    )(grads, loss_tile, mom_attn, mom_mlp)
 
 
 def noise_scalars(level):
@@ -157,9 +679,14 @@
     width = w_attn.shape[1]
     both = ("node", "zero")
 
-    attn_full = lax.all_gather(w_attn.astype(bf16), both, axis=0, tiled=True)
-    mlp_full = lax.all_gather(w_mlp.astype(bf16), both, axis=0, tiled=True)
-    small_full = lax.all_gather(w_small.astype(bf16), both, axis=0, tiled=True)
+    nodes, zeros = lax.axis_size("node"), lax.axis_size("zero")
+    devices = nodes * zeros
+    attn_rows, mlp_rows, small_rows = w_attn.shape[0], w_mlp.shape[0], w_small.shape[0]
+    gathered = gather_weights(nodes, zeros, w_attn, w_mlp, w_small, 1)
+    start = attn_rows + mlp_rows
+    attn_full = gathered[:, :attn_rows].reshape(-1, width)
+    mlp_full = gathered[:, attn_rows:start].reshape(-1, width)
+    small_full = gathered[:, start : start + small_rows].reshape(-1, width)
     half = mlp_full.shape[0] // 2
     w_query, w_output = attn_full[: 3 * width], attn_full[3 * width :]
     w_upper, w_down = mlp_full[:half], mlp_full[half:]
@@ -279,36 +806,45 @@
     g_cond = jnp.einsum("f,jd->jfd", features.astype(f32), grad_modulation).reshape(-1, width)
     g_enc = dot_tn(mixed_high, grad_in) + dot_tn(mixed_low, grad_in)
 
-    local = (
-        jnp.concatenate([g_query, g_output], axis=0),
-        jnp.concatenate([g_upper, g_down], axis=0),
-        jnp.concatenate([g_enc, g_dec, g_cond], axis=0),
-    )
-    g_attn, g_mlp = [
-        lax.psum_scatter(item.astype(bf16), both, scatter_dimension=0, tiled=True).astype(f32)
-        for item in local[:2]
+    small_local = split(jnp.concatenate([g_enc, g_dec, g_cond], axis=0))
+    packed_grads = [
+        jnp.concatenate([g_query, g_output], axis=0).astype(bf16).reshape(devices, attn_rows, width),
+        jnp.concatenate([g_upper, g_down], axis=0).astype(bf16).reshape(devices, mlp_rows, width),
+        small_local[0].reshape(devices, small_rows, width),
+        small_local[1].reshape(devices, small_rows, width),
     ]
-    g_small = lax.psum_scatter(local[2], both, scatter_dimension=0, tiled=True)
-
-    squares = jnp.sum(g_attn * g_attn) + jnp.sum(g_mlp * g_mlp) + jnp.sum(g_small * g_small)
-    total_sq, loss = lax.psum((squares, loss_here), both)
-    clip_norm = jnp.sqrt(total_sq)
+    packed_rows = start + 2 * small_rows
+    packed_grads.append(jnp.zeros((devices, -packed_rows % 16, width), bf16))
+    local = jnp.concatenate(packed_grads, axis=1)
+
+    g_small, moment_attn, moment_mlp, totals, moments = reduce_and_gather(
+        nodes,
+        zeros,
+        local,
+        jnp.full((8, 128), loss_here),
+        mom_attn,
+        mom_mlp,
+        small_rows,
+        2,
+    )
+    loss = totals[4, 0]
+    clip_norm = jnp.sqrt(totals[0, 0])
     factor = jnp.minimum(1.0, clip_limit / clip_norm)
-    moment_attn = moment_decay * mom_attn + factor * g_attn
-    moment_mlp = moment_decay * mom_mlp + factor * g_mlp
 
     flat_index = lax.axis_index(both)
-    full_rows = lax.axis_size(both)
     attn_upper = (flat_index * w_attn.shape[0] >= 3 * width).astype(f32)
     mlp_upper = (flat_index * w_mlp.shape[0] >= half).astype(f32)
-    attn_all = lax.all_gather(moment_attn.astype(bf16), both, axis=0, tiled=True)
-    mlp_all = lax.all_gather(moment_mlp.astype(bf16), both, axis=0, tiled=True)
+    attn_all = moments[:, :attn_rows].reshape(-1, width)
+    mlp_half = lax.dynamic_slice_in_dim(
+        moments, jnp.where(mlp_upper > 0.5, devices // 2, 0), devices // 2, axis=0
+    )
+    low = sixteens(attn_rows)
+    mlp_mine = mlp_half[:, low : low + mlp_rows].reshape(-1, width)
     gram_attn = jnp.where(
         attn_upper > 0.5,
         dot_tn(attn_all[3 * width :], attn_all[3 * width :]),
         dot_tn(attn_all[: 3 * width], attn_all[: 3 * width]),
     )
-    mlp_mine = jnp.where(mlp_upper > 0.5, mlp_all[half:], mlp_all[:half])
     gram_mlp = dot_tn(mlp_mine, mlp_mine)
     attn_factor = jnp.where(attn_upper > 0.5, 0.2 * math.sqrt(width), 0.2 * math.sqrt(3 * width))
     mlp_factor = 0.2 * math.sqrt(max(half, width))

time: 895 us -> 406 us (0.45)
  waiting for transfers between devices: 523 us -> 0.03 us
  Pallas kernels: 0 us -> 133 us
  blocking collectives: 123 us -> 12.2 us
  local copies, waits for them, and re-layouts: 30 us -> 44.4 us
    reduce_scatter x3 -> x0, waiting for transfers between devices: 390 us -> none  [the longest x2 276 us: on_device(): lax.psum_scatter(item.astype(bf16), both, scatter_dimension=0, tiled=True)]
    pallas_call x0 -> x2, Pallas kernels: none -> 133 us  [the longest x1 90.6 us: reduce_and_gather(): pl.pallas_call(kernel, out_shape=(jax.ShapeDtypeStruct((small_rows, width...]
    all_gather x4 -> x0, waiting for transfers between devices: 130 us -> none  [the longest x1 53.9 us: on_device(): lax.all_gather(moment_attn.astype(bf16), both, axis=0, tiled=True)]
    all_gather x1 -> x0, blocking collectives: 73.9 us -> none  [on_device(): small_full = lax.all_gather(w_small.astype(bf16), both, axis=0, tiled=True)]
    psum x1 -> x0, blocking collectives: 36.9 us -> none  [on_device(): total_sq, loss = lax.psum((squares, loss_here), both)]
    slice x0 -> x5, local copies, waits for them, and re-layouts: none -> 11.9 us  [the longest x2 4.8 us: on_device(): w_query, w_output = (attn_full[:3 * width], attn_full[3 * width:])]
    unnamed x249 -> x219, local copies, waits for them, and re-layouts: 16.3 us -> 19.1 us
  transfers between devices with their start and end apart: 12 -> 5, of which waited for: 7 -> 0; matrix products, arithmetic and copies ran while one was open for 10% -> 13% of each run, Pallas kernels for 0% -> 0%
where the time goes in v2:
time: 406 us; the launch traced here: 398 us
  Pallas kernels  133 us (33%)
  matrix products  127 us (31%)
  other arithmetic  57.1 us (14%)
  local copies, waits for them, and re-layouts  44.4 us (11%)
  between operations  20.9 us (5%)
  blocking collectives  12.2 us (3%)
    dot_general x55, matrix products, dot(): lax.dot_general(left, right, (contract, ((), ())), preferred_element_type...  95.1 us
    pallas_call x1, Pallas kernels, reduce_and_gather(): pl.pallas_call(kernel, out_shape=(jax.ShapeDtypeStruct((small_rows, width...  90.6 us
    pallas_call x1, Pallas kernels, gather_weights(): pl.pallas_call(kernel, out_shape=jax.ShapeDtypeStruct((nodes * zeros, row...  42.6 us
    unnamed x219, local copies, waits for them, and re-layouts  19.1 us
    reduce_sum x3, other arithmetic, counted(): return jnp.sum(hits.astype(f32), axis=1)  13.6 us
    all_gather x1, blocking collectives, on_device(): all_parts = lax.all_gather(parts.astype(bf16), 'node', axis=1, tiled=True)  12.2 us
    dot_general x6, matrix products, ns_apply(): squared = jnp.dot(current, current, precision=mid_precision)  8.72 us
  transfers between devices with their start and end apart: 5, of which 0 were waited for; matrix products, arithmetic and copies ran while one was open for 13% of the time, Pallas kernels for 0%

profile of v2, /device:TPU:0, one launch (start us, length us, event | category | flops | bytes accessed | tf_op | source)
XLA Modules:
  0.0 397.8 jit_solution(6020842172405016814)
XLA Ops:
  9.8 42.6 %shard_map.292 = bf16[32,208,512]{2,1,0:T(8,128)(2,1)} custom-call(f32[64,512]{1,0:T(8,128)S(1)} %copy-done.2, f32[128,512]{1,0:T(8,128)S(1)} %copy-done, f32[16,512]{1,0:T(8,128)S(1)} %copy-done.4), custom_call_target="tpu_custom_call" | custom-call | tf_op jit(solution)/shard_map/pallas_call | solution.py:207
  53.6 2.9 slice.163
  58.3 4.9 %convert_reduce_fusion.1 = f32[768,1440]{0,1:T(8,128)} fusion(s32[768,4]{0,1:T(4,128)S(1)} %copy-done.84), kind=kLoop, calls=%fused_computation.2 | loop fusion | flops 12165120 | bytes 4435968 | tf_op jit(solution)/shard_map/reduce_sum | solution.py:611
  64.1 3.1 fusion.16
  77.0 1.9 slice.179
  78.9 4.7 %fusion.170 = (bf16[16,128,512]{2,1,0:T(8,128)(2,1)}, bf16[16,128,512]{2,1,0:T(8,128)(2,1)}) fusion(bf16[32,208,512]{2,1,0:T(8,128)(2,1)} %shard_map.292), kind=kLoop, calls=%fused_computation.313 | loop fusion | bytes 8388608 | tf_op jit(solution)/shard_map/slice | solution.py:692
  84.4 6.1 %convert_reduce_fusion = f32[768,960]{0,1:T(8,128)S(1)} fusion(s32[768,16]{0,1:T(8,128)S(1)} %copy-done.77), kind=kLoop, calls=%fused_computation | loop fusion | flops 34652160 | bytes 2998272 | tf_op jit(solution)/shard_map/reduce_sum | solution.py:611
  91.9 2.5 convert_reduce_fusion.2
  94.5 1.9 pad_maximum_fusion.3
  100.1 2.1 multiply_reduce_fusion.8
  102.2 2.6 multiply_convert_fusion.13
  110.1 2.1 fusion.168
  112.2 4.1 %convolution_add_fusion.4 = f32[768,512]{0,1:T(8,128)S(1)} fusion(f32[768,512]{0,1:T(8,128)S(1)} %get-tuple-element.70, bf16[2048,512]{1,0:T(8,128)(2,1)S(1)} %bitcast.171, f32[768,2048]{1,0:T(8,128)S(1)} %fusion.168), kind=kOutput, calls=%fused_computation.96 | convolution fusion | flops 1625161728 | bytes 11534336 | tf_op jit(solution)/shard_map/dot_general | solution.py:589
  119.7 3.1 fusion.179
  123.2 12.2 %all_gather.7 = bf16[2,16,83,181]{3,0,2,1:T(2,128)(2,1)S(1)} all-gather(bf16[2,4,83,181]{3,0,2,1:T(2,128)(2,1)S(1)} %copy.147), channel_id=1, replica_groups=mesh['node'=4,'zero'=8] {'node'}, dimensions={1}, use_global_device_ids=true | all-gather | bytes 1201840 | tf_op jit(solution)/shard_map/all_gather | solution.py:757
  135.4 1.9 copy_convert_fusion
  137.3 5.5 %fusion.45 = f32[4,16,181]{1,0,2:T(4,128)S(1)} fusion(f32[4,181,181]{2,0,1:T(4,128)} %param.29, f32[16,181,181]{2,1,0:T(8,128)} %all-gather.2.cloned.1.call-done), kind=kOutput, calls=%fused_computation.140 | convolution fusion | flops 25160448 | bytes 2667216 | tf_op jit(solution)/shard_map/tml,uml->tum/dot_general | solution.py:759
  143.0 4.8 %multiply_reduce_fusion = f32[2,4,83,181]{3,2,1,0:T(8,128)S(1)} fusion(f32[2,16,83,181]{3,1,2,0:T(8,128)} %copy_convert_fusion, f32[4,16,181]{2,1,0:T(8,128)S(1)} %copy.142), kind=kLoop, calls=%fused_computation.6 | loop fusion | flops 3725704 | bytes 2450016 | tf_op jit(solution)/shard_map/reduce_sum | solution.py:760
  149.8 2.1 convolution_multiply_fusion.14
  154.8 8.6 %fusion.6 = bf16[768,2048]{1,0:T(8,128)(2,1)S(1)} fusion(f32[768,2048]{1,0:T(8,128)} %copy-done.103, bf16[2048,512]{1,0:T(8,128)(2,1)S(1)} %bitcast.172, f32[768,512]{0,1:T(8,128)S(1)} %convolution_add_fusion.2), kind=kOutput, calls=%fused_computation.16 | convolution fusion | flops 1642463232 | bytes 13107200 | tf_op jit(solution)/shard_map/dot_general | solution.py:589
  163.5 3.8 convolution_convert_fusion.1
  167.2 2.9 fusion.180
  170.2 3.5 convolution_convert_fusion.2
  173.7 3.1 copy.153
  176.8 2.6 multiply_reduce_fusion.12
  179.6 2.0 multiply_add_fusion
  188.1 4.3 %multiply_reduce_fusion.1 = (f32[768]{0:T(1024)S(1)}, f32[768]{0:T(1024)S(1)}, f32[768]{0:T(1024)S(1)}, f32[768]{0:T(1024)S(1)}, f32[768,960]{0,1:T(8,128)}) fusion(f32[768,960]{0,1:T(8,128)S(1)} %convert_reduce_fusion, f32[768]{0:T(1024)S(1)} %get-tuple-element.31, f32[768,960]{0,1:T(8,128)S(1)} %copy-done.10, f32[768]{0:T(1024)S(1)} %get-tuple-element.63, ...), kind=kOutput, calls=%fused_computation.31 | convolution fusion | flops 203486208 | bytes 27029504 | tf_op jit(solution)/shard_map/dot_general | solution.py:589
  192.4 5.2 %multiply_convert_fusion.2 = (bf16[768,960]{0,1:T(8,128)(2,1)S(1)}, bf16[768,960]{0,1:T(8,128)(2,1)}, bf16[768,960]{0,1:T(8,128)(2,1)}) fusion(f32[768,960]{0,1:T(8,128)S(1)} %convert_reduce_fusion, f32[768,960]{0,1:T(8,128)} %get-tuple-element.75, f32[768]{0:T(1024)S(1)} %get-tuple-element.26, f32[768]{0:T(1024)S(1)} %get-tuple-element.31, ...), kind=kLoop, calls=%fused_computation.29 | loop fusion | flops 17694720 | bytes 25095168 | tf_op jit(solution)/shard_map/convert_element_type | solution.py:791
  197.6 3.1 fusion.48
  200.6 2.8 fusion.41
  204.2 1.9 multiply_convert_fusion.6
  207.2 2.6 fusion.50
  209.8 1.8 fusion.49
  213.7 2.7 fusion.40
  216.4 2.9 fusion.39
  226.3 2.6 convert.63
  232.0 4.1 %pad_maximum_fusion.1 = bf16[4096,512]{1,0:T(8,128)(2,1)} fusion(bf16[2048,512]{1,0:T(8,128)(2,1)S(1)} %copy-done.61, bf16[2048,512]{1,0:T(8,128)(2,1)} %convolution_convert_fusion.2), kind=kLoop, calls=%fused_computation.19 | loop fusion | flops 8388608 | bytes 8388608 | tf_op jit(solution)/shard_map/concatenate | solution.py:812
  240.1 2.5 fusion.181
  242.6 2.7 convolution_convert_fusion.3
  245.3 1.9 copy.158
  249.3 2.0 add_convert_fusion
  253.9 2.0 copy-done.21
  256.0 3.5 pad_maximum_fusion.grads_ref
  260.0 90.6 %shard_map.293 = (f32[16,512]{1,0:T(8,128)}, f32[64,512]{1,0:T(8,128)}, f32[128,512]{1,0:T(8,128)}, f32[8,128]{1,0:T(8,128)}, bf16[32,192,512]{2,1,0:T(8,128)(2,1)}) custom-call(bf16[32,224,512]{2,1,0:T(8,128)(2,1)} %pad_maximum_fusion.grads_ref, f32[8,128]{1,0:T(8,128)} %broadcast_in_dim.24.loss_ref, f32[64,512]{1,0:T(8,128)} %attn_ref.3, f32[128,512]{1,0:T(8,128)} %mlp_ref.3), custom_call_target="tpu_custom_call" | custom-call | tf_op jit(solution)/shard_map/pallas_call | solution.py:536
  350.7 4.1 %select_reduce_fusion = (f32[]{:T(128)}, f32[512,512]{1,0:T(8,128)S(1)}) fusion(bf16[32,192,512]{2,1,0:T(8,128)(2,1)} %get-tuple-element.19, s32[]{:T(128)S(6)} %select_n.55, s32[]{:T(128)S(6)} %add.208), kind=kOutput, calls=%fused_computation.157 | convolution fusion | flops 1074528256 | bytes 3145740 | tf_op jit(solution)/shard_map/dot_general | solution.py:589
  360.4 4.5 %select_reduce_fusion.1 = (f32[]{:T(128)}, f32[512,512]{1,0:T(8,128)}) fusion(f32[512,512]{1,0:T(8,128)S(1)} %convolution_bitcast_fusion, bf16[32,192,512]{2,1,0:T(8,128)(2,1)} %get-tuple-element.19, pred[]{:T(512)S(6)} %gt.15), kind=kOutput, calls=%fused_computation.158 | convolution fusion | flops 806354944 | bytes 3670021 | tf_op jit(solution)/shard_map/dot_general | solution.py:589
  365.6 3.1 fusion.34
  368.8 2.1 fusion.58
  (332 shorter events, 86.6 us)
Async XLA Ops:
  7.2 130.1 %all-gather.2.cloned.1.call-start = ((), (), s32[]{:S(2)}) async-start(), calls=%async_computation | async-start | bytes 3768320 | tf_op jit(solution)/shard_map/all_gather | solution.py:758
  52.4 4.9 %copy-start.65 = (bf16[1,4,360,261]{2,1,3,0:T(4,128)(2,1)S(1)}, bf16[1,4,360,261]{2,1,3,0:T(4,128)(2,1)}, u32[]{:S(2)}) copy-start(bf16[1,4,360,261]{2,1,3,0:T(4,128)(2,1)} %param.21) | copy-start | bytes 2255044
  53.6 63.0 %copy-start.49 = (bf16[32,16,512]{2,1,0:T(8,128)(2,1)}, bf16[32,16,512]{2,1,0:T(8,128)(2,1)S(1)}, u32[]{:S(2)}) copy-start(bf16[32,16,512]{2,1,0:T(8,128)(2,1)S(1)} %slice.158) | copy-start | bytes 1572868
  53.6 4.7 %copy-start.84 = (s32[768,4]{0,1:T(4,128)S(1)}, s32[768,4]{0,1:T(4,128)}, u32[]{:S(2)}) copy-start(s32[768,4]{0,1:T(4,128)} %param.27) | copy-start | bytes 36868
  64.1 4.6 %copy-start.86 = (f32[1,512]{1,0:T(1,128)}, f32[1,512]{1,0:T(1,128)S(1)}, u32[]{:S(2)}) copy-start(f32[1,512]{1,0:T(1,128)S(1)} %get-tuple-element.55) | copy-start | bytes 6148
  70.9 12.7 %copy-start.32 = (bf16[768,1536]{1,0:T(8,128)(2,1)}, bf16[768,1536]{1,0:T(8,128)(2,1)S(1)}, u32[]{:S(2)}) copy-start(bf16[768,1536]{1,0:T(8,128)(2,1)S(1)} %convolution_convert_fusion) | copy-start | bytes 7077892
  72.1 22.4 %collective-permute-start.1 = (bf16[96,1024]{1,0:T(8,128)(2,1)}, bf16[96,1024]{1,0:T(8,128)(2,1)}, u32[]{:S(2)}, u32[]{:S(2)}) collective-permute-start(bf16[96,1024]{1,0:T(8,128)(2,1)} %convolution_convert_fusion.10), channel_id=1, source_target_pairs={{0,24},{8,0},{16,8},{24,16},{1,25},{9,1},{17,9},{25,17},{2,26},{10... | collective-permute-start | bytes 589832 | tf_op jit(solution)/shard_map/ppermute | solution.py:617
  72.8 21.6 %collective-permute-start = (bf16[96,1024]{1,0:T(8,128)(2,1)}, bf16[96,1024]{1,0:T(8,128)(2,1)}, u32[]{:S(2)}, u32[]{:S(2)}) collective-permute-start(bf16[96,1024]{1,0:T(8,128)(2,1)} %convolution_convert_fusion.10), channel_id=1, source_target_pairs={{0,8},{8,16},{16,24},{24,0},{1,9},{9,17},{17,25},{25,1},{2,10},{10... | collective-permute-start | bytes 589832 | tf_op jit(solution)/shard_map/ppermute | solution.py:617
  94.4 23.3 %copy-start.6 = (bf16[1440,768]{1,0:T(8,128)(2,1)}, bf16[1440,768]{1,0:T(8,128)(2,1)S(1)}, u32[]{:S(2)}) copy-start(bf16[1440,768]{1,0:T(8,128)(2,1)S(1)} %convert_reduce_fusion.2) | copy-start | bytes 6635524
  94.4 2.9 copy-start.33
  97.3 9.5 %copy-start.30 = (bf16[960,1024]{1,0:T(8,128)(2,1)}, bf16[960,1024]{1,0:T(8,128)(2,1)S(1)}, u32[]{:S(2)}) copy-start(bf16[960,1024]{1,0:T(8,128)(2,1)S(1)} %pad_maximum_fusion.3) | copy-start | bytes 5898244
  98.0 4.2 %copy-start.9 = (f32[768,960]{0,1:T(8,128)}, f32[768,960]{0,1:T(8,128)S(1)}, u32[]{:S(2)}) copy-start(f32[768,960]{0,1:T(8,128)S(1)} %get-tuple-element.64) | copy-start | bytes 8847364
  98.7 3.5 copy-start.11
  99.4 2.8 copy-start.7
  105.7 3.4 copy-start.97
  105.7 2.8 copy-start.55
  109.2 3.1 copy-start.22
  112.2 4.1 %copy-start.103 = (f32[768,2048]{1,0:T(8,128)}, f32[768,2048]{1,0:T(8,128)S(1)}, u32[]{:S(2)}) copy-start(f32[768,2048]{1,0:T(8,128)S(1)} %fusion.168) | copy-start | bytes 18874372
  142.8 5.8 %copy-start.93 = (f32[83]{0:T(128)S(1)}, f32[83]{0:T(128)}, u32[]{:S(2)}) copy-start(f32[83]{0:T(128)} %compare_convert_fusion) | copy-start | bytes 1000
  143.0 5.6 %copy-start.94 = (f32[2,360,181,1]{1,2,0,3:T(8,128)S(1)}, f32[2,360,181,1]{1,2,0,3:T(8,128)}, u32[]{:S(2)}) copy-start(f32[2,360,181,1]{1,2,0,3:T(8,128)} %constant.151) | copy-start | bytes 1563844
  151.9 2.9 copy-start.60
  153.3 10.1 %slice-start.1 = ((s8[6291456]{0:T(1024)(128)(4,1)}), s8[4194304]{0:T(1024)(128)(4,1)S(1)}, s32[]{:S(2)}) async-start(s8[6291456]{0:T(1024)(128)(4,1)} %bitcast.192), calls=%async_computation.2 | async-start | bytes 8388608
  154.8 8.6 %copy-start.36 = (f32[768,512]{0,1:T(8,128)}, f32[768,512]{0,1:T(8,128)S(1)}, u32[]{:S(2)}) copy-start(f32[768,512]{0,1:T(8,128)S(1)} %convolution_add_fusion.2) | copy-start | bytes 4718596
  154.8 8.6 %slice-start.2 = ((s8[6291456]{0:T(1024)(128)(4,1)}), s8[2097152]{0:T(1024)(128)(4,1)S(1)}, s32[]{:S(2)}) async-start(s8[6291456]{0:T(1024)(128)(4,1)} %bitcast.192), calls=%async_computation.3 | async-start | bytes 4194304
  163.5 3.8 copy-start.58
  167.2 3.0 copy-start.23
  167.2 3.0 copy-start.89
  176.8 2.8 copy-start.25
  185.2 2.9 copy-start.8
  192.4 8.3 %copy-start.34 = (bf16[768,1536]{1,0:T(8,128)(2,1)S(1)}, bf16[768,1536]{1,0:T(8,128)(2,1)}, u32[]{:S(2)}) copy-start(bf16[768,1536]{1,0:T(8,128)(2,1)} %copy-done.32) | copy-start | bytes 7077892
  197.6 8.5 %copy-start.47 = (bf16[768,960]{0,1:T(8,128)(2,1)}, bf16[768,960]{0,1:T(8,128)(2,1)S(1)}, u32[]{:S(2)}) copy-start(bf16[768,960]{0,1:T(8,128)(2,1)S(1)} %get-tuple-element.44) | copy-start | bytes 4423684
  197.6 5.8 %copy-start.52 = (f32[2,4,83,181]{3,2,1,0:T(8,128)S(1)}, f32[2,4,83,181]{3,2,1,0:T(8,128)}, u32[]{:S(2)}) copy-start(f32[2,4,83,181]{3,2,1,0:T(8,128)} %get-tuple-element.72) | copy-start | bytes 1442212
  197.6 5.8 %copy-start.54 = (f32[2,4,83,181]{3,2,1,0:T(8,128)S(1)}, f32[2,4,83,181]{3,2,1,0:T(8,128)}, u32[]{:S(2)}) copy-start(f32[2,4,83,181]{3,2,1,0:T(8,128)} %copy-done.53) | copy-start | bytes 1442212
  207.2 6.5 %copy-start.35 = (bf16[768,1536]{1,0:T(8,128)(2,1)S(1)}, bf16[768,1536]{1,0:T(8,128)(2,1)}, u32[]{:S(2)}) copy-start(bf16[768,1536]{1,0:T(8,128)(2,1)} %copy-done.32) | copy-start | bytes 7077892
  212.9 6.4 %copy-start.48 = (bf16[768,960]{0,1:T(8,128)(2,1)S(1)}, bf16[768,960]{0,1:T(8,128)(2,1)}, u32[]{:S(2)}) copy-start(bf16[768,960]{0,1:T(8,128)(2,1)} %copy-done.47) | copy-start | bytes 4423684
  216.4 4.3 %copy-start.38 = (bf16[768,512]{1,0:T(8,128)(2,1)S(1)}, bf16[768,512]{1,0:T(8,128)(2,1)}, u32[]{:S(2)}) copy-start(bf16[768,512]{1,0:T(8,128)(2,1)} %copy-done.37) | copy-start | bytes 2359300
  216.4 4.3 %copy-start.46 = (bf16[768,960]{0,1:T(8,128)(2,1)S(1)}, bf16[768,960]{0,1:T(8,128)(2,1)}, u32[]{:S(2)}) copy-start(bf16[768,960]{0,1:T(8,128)(2,1)} %copy-done.45) | copy-start | bytes 4423684
  219.3 2.8 copy-start.44
  220.7 2.8 copy-start.42
  222.1 2.7 copy-start.40
  226.3 5.7 %copy-start.61 = (bf16[2048,512]{1,0:T(8,128)(2,1)S(1)}, bf16[2048,512]{1,0:T(8,128)(2,1)}, u32[]{:S(2)}) copy-start(bf16[2048,512]{1,0:T(8,128)(2,1)} %convolution_convert_fusion.1) | copy-start | bytes 6291460
  229.5 8.4 %collective-permute-start.3 = (bf16[96,1024]{1,0:T(8,128)(2,1)S(1)}, bf16[96,1024]{1,0:T(8,128)(2,1)}, u32[]{:S(2)}, u32[]{:S(2)}) collective-permute-start(bf16[96,1024]{1,0:T(8,128)(2,1)S(1)} %get-tuple-element.51), channel_id=1, source_target_pairs={{0,8},{8,16},{16,24},{24,0},{1,9},{9,17},{17,25},{25,1},{2,10},{10... | collective-permute-start | bytes 589832 | tf_op jit(solution)/shard_map/ppermute | solution.py:617
  229.9 7.4 %collective-permute-start.2 = (bf16[96,1024]{1,0:T(8,128)(2,1)}, bf16[96,1024]{1,0:T(8,128)(2,1)S(1)}, u32[]{:S(2)}, u32[]{:S(2)}) collective-permute-start(bf16[96,1024]{1,0:T(8,128)(2,1)} %get-tuple-element.52), channel_id=1, source_target_pairs={{0,24},{8,0},{16,8},{24,16},{1,25},{9,1},{17,9},{25,17},{2,26},{10... | collective-permute-start | bytes 589832 | tf_op jit(solution)/shard_map/ppermute | solution.py:617
  231.9 4.1 %copy-start.83 = (bf16[768,1536]{1,0:T(8,128)(2,1)S(1)}, bf16[768,1536]{1,0:T(8,128)(2,1)}, u32[]{:S(2)}) copy-start(bf16[768,1536]{1,0:T(8,128)(2,1)} %constant_dynamic-update-slice_fusion.3) | copy-start | bytes 7077892
  231.9 4.2 %copy-start.27 = (f32[768,512]{0,1:T(8,128)S(1)}, f32[768,512]{0,1:T(8,128)}, u32[]{:S(2)}) copy-start(f32[768,512]{0,1:T(8,128)} %copy-done.26) | copy-start | bytes 4718596
  365.6 3.2 copy-start.67
  365.6 5.2 %copy-start.71 = (f32[64,512]{1,0:T(8,128)S(1)}, f32[64,512]{1,0:T(8,128)}, u32[]{:S(2)}) copy-start(f32[64,512]{1,0:T(8,128)} %get-tuple-element.105) | copy-start | bytes 393220
  384.9 3.1 copy-start.72
  (64 other events, 117.7 us)
Sparse Core Ops, SparseCore 0:
  74.2 31.3 all-gather.1
